TPU v7x, 32 devices: a whole 2x2x4 slice. The times are simulated.
32 devices in a mesh: seq: 4 (over y, core), ctx: 8 (over z, x).
Axes of the slice: x: 2, y: 2, z: 4, core: 2. Of those that a mesh axis runs over, the one named last changes fastest.
Arguments:
- inputs: bfloat16 [24576, 1024], P(('seq', 'ctx')), parts along dimension 0, may hold values from -9 to 9
- qkv_weight: bfloat16 [1024, 3072], replicated, may hold values from -3 to 3
- out_weight: bfloat16 [1024, 1024], replicated, may hold values from -0.1875 to 0.1875
- rand_owner: int32 [384, 3], P(('seq', 'ctx')), parts along dimension 0, may hold values from 0 to 7, all different within a row; in each aligned block of 12 rows (0 to 11, 12 to 23, ...) at most 5 rows name the same one
- rand_local: int32 [384, 3], P(('seq', 'ctx')), parts along dimension 0, may hold values from 0 to 11
Outputs:
- attended: bfloat16 [24576, 1024], P(('seq', 'ctx')), parts along dimension 0
There are 4 independent parts, one for each index of `seq`. A program takes and returns all parts, laid end to end along the dimension named above; an argument that names none is the same for every part. Nothing has to cross between parts.
Inputs may be any that keep to these rules, and one draw needn't show every extreme that they name: `rand_owner`: within the 12 rows of one device no owner is named by more than 5 rows, a bound that some block reaches; the 3 owners of one row differ. Rows of the first and the last block are not used.
All inputs are finite; a program needn't handle non-finite values.
Results may differ from a plain program's by a relative error of at most 0.003.
The roundings to bfloat16 on the way count: a program that leaves them out, or rounds other values in their place, can miss the bound.
Values may be sent and summed in bfloat16 or wider, within the bound.
A program may use at most 192 MiB of HBM per device.

v0:
```python
import math

import jax
import jax.numpy as jnp
from jax import lax
from jax.sharding import PartitionSpec as P

HEADS = 16
BLOCK = 64


def from_root(shard, axis, root):
    mine = lax.axis_index(axis) == root
    return lax.psum(jnp.where(mine, shard, jnp.zeros_like(shard)), axis)


def padded(shard, sides, width):
    for axis, dim in sides:
        devices, length = (lax.axis_size(axis), shard.shape[dim])
        up = [(i, (i + 1) % devices) for i in range(devices - 1)]
        down = [(j, i) for i, j in up]
        last = lax.slice_in_dim(shard, length - width, length, axis=dim)
        initial = lax.slice_in_dim(shard, 0, width, axis=dim)
        before = lax.ppermute(last, axis, up)
        after = lax.ppermute(initial, axis, down)
        shard = jnp.concatenate([before, shard, after], axis=dim)
    return shard


def combined_all(value, axis, join):
    pieces = jax.tree.map(lambda part: lax.all_gather(part, axis), value)
    head = jax.tree.map(lambda part: part[0], pieces)
    tail = jax.tree.map(lambda part: part[1:], pieces)
    total, _ = lax.scan(lambda total, section: (join(total, section), None), head, tail)
    return total


def request_slots(owners, n_dev, capacity):
    flat_owner = owners.reshape(-1)
    onehot = (flat_owner[:, None] == jnp.arange(n_dev, dtype=jnp.int32)[None, :]).astype(jnp.int32)
    before = jnp.cumsum(onehot, axis=0) - onehot
    rank_of = jnp.sum(before * onehot, axis=1)
    return flat_owner * capacity + rank_of


def combine_partial(partial_a, partial_b):
    row_top = jnp.maximum(partial_a[0], partial_b[0])
    factor_a = jnp.exp(partial_a[0] - row_top)
    factor_b = jnp.exp(partial_b[0] - row_top)
    denom_sum = partial_a[1] * factor_a + partial_b[1] * factor_b
    numerator = partial_a[2] * factor_a[..., None] + partial_b[2] * factor_b[..., None]
    return (row_top, denom_sum, numerator)


def per_device(inputs, qkv_weight, out_weight, rand_owner, rand_local):
    tok_rows, width = inputs.shape
    head_dim = width // HEADS
    inv_root = 1.0 / math.sqrt(head_dim)
    n_local = tok_rows // BLOCK
    n_dev = lax.axis_size("ctx")
    device_index = lax.axis_index("ctx")
    capacity = max(2, (3 * n_local + n_dev - 1) // n_dev)
    projected = jnp.dot(inputs, qkv_weight, preferred_element_type=jnp.float32).astype(jnp.bfloat16)
    queries = projected[:, :width]
    key_value = projected[:, width:]
    first_rows = from_root(projected[:BLOCK], "ctx", 0)
    last_rows = from_root(projected[tok_rows - BLOCK :], "ctx", n_dev - 1)
    global_rows = jnp.concatenate([first_rows, last_rows], axis=0)
    rimmed = padded(key_value, (("ctx", 0),), BLOCK)
    slot_ids = request_slots(rand_owner, n_dev, capacity)
    wanted = rand_local.reshape(-1)
    request_table = jnp.zeros((n_dev * capacity,), jnp.int32).at[slot_ids].set(wanted)
    asked_for = lax.all_to_all(
        request_table.reshape(n_dev, capacity), "ctx", split_axis=0, concat_axis=0, tiled=True
    )
    source = key_value.reshape(n_local, BLOCK, 2 * width)
    outgoing = source[asked_for]
    arrived = lax.all_to_all(outgoing, "ctx", split_axis=0, concat_axis=0, tiled=True)
    picked = arrived.reshape(n_dev * capacity, BLOCK, -1)[slot_ids]
    rand_kv = picked.reshape(n_local, 3, BLOCK, 2 * width)
    n_blocks = n_local * n_dev
    block_ids = device_index * n_local + jnp.arange(n_local, dtype=jnp.int32)
    rand_ids = rand_owner * n_local + rand_local
    window_ids = jnp.stack([block_ids - 1, block_ids, block_ids + 1], axis=1)
    global_ids = jnp.broadcast_to(jnp.array([0, n_blocks - 1], jnp.int32), (n_local, 2))
    fixed_ids = jnp.concatenate([window_ids, global_ids], axis=1)
    window_ok = jnp.stack(
        [block_ids - 1 >= 1, block_ids >= 0, block_ids + 1 < n_blocks - 1], axis=1
    )
    rand_ok = jnp.all(rand_ids[:, :, None] != fixed_ids[:, None, :], axis=2)
    usable = jnp.concatenate([window_ok, jnp.ones((n_local, 2), bool), rand_ok], axis=1)
    padded_blocks = rimmed.reshape(n_local + 2, BLOCK, 2 * width)
    glob_kv = global_rows[:, width:].reshape(2, BLOCK, 2 * width)
    query_blocks = queries.reshape(n_local, BLOCK, HEADS, head_dim)
    group_size = math.gcd(n_local, 8)

    def attend(group_index):
        first_block = group_index * group_size
        near_blocks = lax.dynamic_slice_in_dim(padded_blocks, first_block, group_size + 2, 0)
        window = jnp.stack([near_blocks[:-2], near_blocks[1:-1], near_blocks[2:]], axis=1)
        remote = lax.dynamic_slice_in_dim(rand_kv, first_block, group_size, 0)
        shared = jnp.broadcast_to(glob_kv[None], (group_size, 2, BLOCK, 2 * width))
        gathered = jnp.concatenate([window, shared, remote], axis=1).reshape(
            group_size, 8 * BLOCK, 2 * width
        )
        group_keys = gathered[:, :, :width].reshape(group_size, 8 * BLOCK, HEADS, head_dim)
        group_values = gathered[:, :, width:].reshape(group_size, 8 * BLOCK, HEADS, head_dim)
        group_queries = lax.dynamic_slice_in_dim(query_blocks, first_block, group_size, 0)
        live_keys = jnp.repeat(
            lax.dynamic_slice_in_dim(usable, first_block, group_size, 0), BLOCK, axis=1
        )
        scores = (
            jnp.einsum(
                "gqhd,gkhd->ghqk", group_queries, group_keys, preferred_element_type=jnp.float32
            )
            * inv_root
        )
        scores = jnp.where(live_keys[:, None, None, :], scores, -jnp.inf)
        row_top = jnp.max(scores, axis=-1, keepdims=True)
        exponent = jnp.exp(scores - row_top)
        weights = (exponent / jnp.sum(exponent, axis=-1, keepdims=True)).astype(jnp.bfloat16)
        mixture = jnp.einsum(
            "ghqk,gkhd->gqhd", weights, group_values, preferred_element_type=jnp.float32
        )
        return mixture.reshape(group_size * BLOCK, width)

    context = lax.map(attend, jnp.arange(n_local // group_size, dtype=jnp.int32)).reshape(
        tok_rows, width
    )
    glob_queries = global_rows[:, :width].reshape(2 * BLOCK, HEADS, head_dim)
    local_keys = key_value[:, :width].reshape(tok_rows, HEADS, head_dim)
    local_values = key_value[:, width:].reshape(tok_rows, HEADS, head_dim).astype(jnp.float32)
    glob_scores = (
        jnp.einsum("qhd,khd->qhk", glob_queries, local_keys, preferred_element_type=jnp.float32)
        * inv_root
    )
    row_top = jnp.max(glob_scores, axis=-1)
    exponent = jnp.exp(glob_scores - row_top[..., None])
    denom_sum = jnp.sum(exponent, axis=-1)
    numerator = jnp.einsum("qhk,khd->qhd", exponent, local_values, precision=lax.Precision.HIGHEST)
    row_top, denom_sum, numerator = combined_all(
        (row_top, denom_sum, numerator), "ctx", combine_partial
    )
    glob_context = (numerator / denom_sum[..., None]).reshape(2 * BLOCK, width)
    lead_rows = jnp.where(device_index == 0, glob_context[:BLOCK], context[:BLOCK])
    tail_rows = jnp.where(
        device_index == n_dev - 1, glob_context[BLOCK:], context[tok_rows - BLOCK :]
    )
    context = jnp.concatenate(
        [lead_rows, context[BLOCK : tok_rows - BLOCK], tail_rows], axis=0
    ).astype(jnp.bfloat16)
    return jnp.dot(context, out_weight, preferred_element_type=jnp.float32).astype(jnp.bfloat16)


def solution(mesh):
    in_specs = (P(("seq", "ctx"), None), P(), P(), P(("seq", "ctx"), None), P(("seq", "ctx"), None))
    out_specs = P(("seq", "ctx"), None)
    return jax.shard_map(
        per_device, mesh=mesh, in_specs=in_specs, out_specs=out_specs, check_vma=False
    )
```

profile of v0, /device:TPU:0, one launch (start us, length us, event | category | flops | bytes accessed | tf_op | source)
XLA Modules:
  0.0 639.8 jit_solution(12290488026576560992)
XLA Ops:
  11.0 7.3 %all-to-all-start = ((s32[8,1,5]{2,1,0:T(1,128)}), s32[8,1,5]{2,1,0:T(1,128)S(1)}, u32[]{:S(2)}, u32[]{:S(2)}) async-start(s32[8,1,5]{2,1,0:T(1,128)} %bitcast.25), calls=%async_computation | async-start | bytes 8192 | tf_op jit(solution)/shard_map/all_to_all | solution.py:73
  18.2 7.6 %convolution_convert_fusion = bf16[768,3072]{1,0:T(8,128)(2,1)S(1)} fusion(bf16[768,1024]{1,0:T(8,128)(2,1)} %param.10, bf16[1024,3072]{1,0:T(8,128)(2,1)} %param.11), kind=kOutput, calls=%fused_computation.42 | convolution fusion | flops 4834197504 | bytes 12582912 | tf_op jit(solution)/shard_map/dot_general | solution.py:63
  30.3 7.4 %gather_fusion = bf16[40,64,2048]{2,1,0:T(8,128)(2,1)} fusion(bf16[12,64,2048]{2,1,0:T(8,128)(2,1)} %bitcast.115, s32[1024]{0:T(1024)S(1)} %pad_clamp_fusion.1), kind=kCustom, calls=%fused_computation | custom fusion | bytes 20971680 | tf_op jit(solution)/shard_map/gather | solution.py:77
  37.7 6.1 all-to-all-start.1
  45.9 4.8 fusion.50
  50.7 2.6 copy.84
  53.3 2.6 copy.86
  55.9 264.4 %all-reduce.3.cloned.1.call-done = (bf16[64,3072]{1,0:T(8,128)(2,1)}, bf16[64,3072]{1,0:T(8,128)(2,1)}) async-done(((bf16[64,3072]{1,0:T(8,128)(2,1)}, bf16[64,3072]{1,0:T(8,128)(2,1)}), (bf16[64,3072]{1,0:T(8,128)(2,1)}, bf16[64,3072]{1,0:T(8,128)(2,1)})) %all-reduce.3.cloned.1.call-update) | async-done | bytes 786448 | tf_op jit(solution)/shard_map/psum | solution.py:14
  322.6 2.7 bitcast_reduce_fusion
  325.3 2.6 copy-done.1
  328.0 4.0 fusion.33
  333.9 2.5 collective-permute-start
  338.2 5.3 reshape.154
  343.5 5.8 collective-permute-done
  351.5 3.4 pad_maximum_fusion
  355.9 33.1 %all-gather.1 = f32[1024,16]{0,1:T(8,128)S(1)} all-gather(f32[128,16]{0,1:T(8,128)S(1)} %fusion.25), channel_id=3, replica_groups=mesh['seq'=4,'ctx'=8] {'ctx'}, dimensions={0}, use_global_device_ids=true | all-gather | bytes 73728 | tf_op jit(solution)/shard_map/all_gather | solution.py:31
  389.0 30.8 %all-gather = f32[1024,16]{0,1:T(8,128)S(1)} all-gather(f32[128,16]{0,1:T(8,128)S(1)} %get-tuple-element.203), channel_id=2, replica_groups=mesh['seq'=4,'ctx'=8] {'ctx'}, dimensions={0}, use_global_device_ids=true | all-gather | bytes 73728 | tf_op jit(solution)/shard_map/all_gather | solution.py:31
  420.7 4.3 slice.134
  425.0 7.6 %copy.102 = f32[896,16,64]{2,1,0:T(8,128)} copy(f32[896,16,64]{0,2,1:T(8,128)} %slice.134) | data formatting | bytes 7340032 | tf_op jit(solution)/shard_map/while | solution.py:34
  436.1 15.1 %while.24 = (s32[]{:T(128)}, f32[128,16]{0,1:T(8,128)S(1)}, f32[128,16]{0,1:T(8,128)S(1)}, f32[128,16,64]{2,1,0:T(8,128)S(1)}, f32[7,128,16]{1,0,2:T(8,128)S(1)}...) while((s32[]{:T(128)}, f32[128,16]{0,1:T(8,128)S(1)}, f32[128,16]{0,1:T(8,128)S(1)}, ...), condition=%wide.region_5.6_spmd, body=%wide.region_4.5_spmd.sunk | while | flops 405506 | bytes 1720413 | solution.py:34
  453.4 9.4 %gather_fusion.1 = bf16[36,64,2048]{2,1,0:T(8,128)(2,1)} fusion(bf16[40,64,2048]{2,1,0:T(8,128)(2,1)} %bitcast.28, s32[1024]{0:T(1024)S(1)} %pad_clamp_fusion), kind=kCustom, calls=%fused_computation.1 | custom fusion | bytes 18874512 | tf_op jit(solution)/shard_map/gather | solution.py:79
  462.8 164.8 %while.25 = (s32[]{:T(128)}, bf16[3,256,1024]{2,1,0:T(8,128)(2,1)}, s32[3]{0:T(128)S(1)}, bf16[14,64,2048]{2,1,0:T(8,128)(2,1)}, bf16[128,2048]{1,0:T(8,128)(2,1...) while((s32[]{:T(128)}, bf16[3,256,1024]{2,1,0:T(8,128)(2,1)}, ...), condition=%wide.region_13.14_spmd, body=%wide.region_10.13_spmd.sunk | while | flops 549454336 | bytes 79209328 | solution.py:127
  466.3 2.3 fusion.77
  468.6 2.3 fusion.78
  470.9 2.6 broadcast_dynamic-update-slice_fusion.2
  473.5 4.0 dynamic-slice_dynamic-update-slice_fusion.2
  477.5 6.1 fusion.79
  483.6 6.2 copy.128
  491.4 7.8 %fusion.80 = (f32[4,16,64]{2,1,0:T(8,128)S(1)}, f32[4,16,64,512]{3,2,1,0:T(8,128)}) fusion(pred[4,512]{1,0:T(4,128)(4,1)S(1)} %broadcast_in_dim.79, bf16[4,512,16,64]{1,3,2,0:T(8,128)(2,1)} %bitcast.112, bf16[4,64,16,64]{3,2,1,0:T(8,128)(2,1)S(1)} %constant_dynamic-slice_fusion.9), kind=kOutput, calls=%fused_computation.88.clone.1 | convolution fusion | flops 276824576 | bytes 13125632 | tf_op jit(solution)/shard_map/while/body/eval_jaxpr/sub | solution.py:120
  499.2 6.2 copy.127
  505.4 7.0 %fusion.81 = bf16[4,64,16,64]{1,3,2,0:T(8,128)(2,1)} fusion(bf16[4,512,16,64]{1,3,2,0:T(8,128)(2,1)} %bitcast.113, f32[4,16,64,512]{3,2,1,0:T(8,128)} %get-tuple-element.319, f32[4,16,64]{2,1,0:T(8,128)S(1)} %get-tuple-element.320), kind=kOutput, calls=%fused_computation.21.clone.1 | convolution fusion | flops 272629760 | bytes 13123584 | tf_op jit(solution)/shard_map/while/body/eval_jaxpr/ghqk,gkhd->gqhd/dot_general | solution.py:122
  521.2 2.3 fusion.77
  525.8 2.6 broadcast_dynamic-update-slice_fusion.2
  528.4 4.0 dynamic-slice_dynamic-update-slice_fusion.2
  532.4 6.1 fusion.79
  538.5 6.2 copy.128
  546.3 7.8 %fusion.80 = (f32[4,16,64]{2,1,0:T(8,128)S(1)}, f32[4,16,64,512]{3,2,1,0:T(8,128)}) fusion(pred[4,512]{1,0:T(4,128)(4,1)S(1)} %broadcast_in_dim.79, bf16[4,512,16,64]{1,3,2,0:T(8,128)(2,1)} %bitcast.112, bf16[4,64,16,64]{3,2,1,0:T(8,128)(2,1)S(1)} %constant_dynamic-slice_fusion.9), kind=kOutput, calls=%fused_computation.88.clone.1 | convolution fusion | flops 276824576 | bytes 13125632 | tf_op jit(solution)/shard_map/while/body/eval_jaxpr/sub | solution.py:120
  554.1 6.2 copy.127
  560.3 7.0 %fusion.81 = bf16[4,64,16,64]{1,3,2,0:T(8,128)(2,1)} fusion(bf16[4,512,16,64]{1,3,2,0:T(8,128)(2,1)} %bitcast.113, f32[4,16,64,512]{3,2,1,0:T(8,128)} %get-tuple-element.319, f32[4,16,64]{2,1,0:T(8,128)S(1)} %get-tuple-element.320), kind=kOutput, calls=%fused_computation.21.clone.1 | convolution fusion | flops 272629760 | bytes 13123584 | tf_op jit(solution)/shard_map/while/body/eval_jaxpr/ghqk,gkhd->gqhd/dot_general | solution.py:122
  576.2 2.3 fusion.77
  580.8 2.6 broadcast_dynamic-update-slice_fusion.2
  583.3 4.0 dynamic-slice_dynamic-update-slice_fusion.2
  587.3 6.1 fusion.79
  593.4 6.2 copy.128
  601.2 7.8 %fusion.80 = (f32[4,16,64]{2,1,0:T(8,128)S(1)}, f32[4,16,64,512]{3,2,1,0:T(8,128)}) fusion(pred[4,512]{1,0:T(4,128)(4,1)S(1)} %broadcast_in_dim.79, bf16[4,512,16,64]{1,3,2,0:T(8,128)(2,1)} %bitcast.112, bf16[4,64,16,64]{3,2,1,0:T(8,128)(2,1)S(1)} %constant_dynamic-slice_fusion.9), kind=kOutput, calls=%fused_computation.88.clone.1 | convolution fusion | flops 276824576 | bytes 13125632 | tf_op jit(solution)/shard_map/while/body/eval_jaxpr/sub | solution.py:120
  609.1 6.2 copy.127
  615.3 7.0 %fusion.81 = bf16[4,64,16,64]{1,3,2,0:T(8,128)(2,1)} fusion(bf16[4,512,16,64]{1,3,2,0:T(8,128)(2,1)} %bitcast.113, f32[4,16,64,512]{3,2,1,0:T(8,128)} %get-tuple-element.319, f32[4,16,64]{2,1,0:T(8,128)S(1)} %get-tuple-element.320), kind=kOutput, calls=%fused_computation.21.clone.1 | convolution fusion | flops 272629760 | bytes 13123584 | tf_op jit(solution)/shard_map/while/body/eval_jaxpr/ghqk,gkhd->gqhd/dot_general | solution.py:122
  630.0 2.9 convolution_convert_fusion.1
  (142 shorter events, 77.7 us)
Async XLA Ops:
  6.5 623.5 %copy-start = (bf16[1024,1024]{1,0:T(8,128)(2,1)S(1)}, bf16[1024,1024]{1,0:T(8,128)(2,1)}, u32[]{:S(2)}) copy-start(bf16[1024,1024]{1,0:T(8,128)(2,1)} %param.12) | copy-start | bytes 6291460
  11.0 19.0 %all-to-all-start = ((s32[8,1,5]{2,1,0:T(1,128)}), s32[8,1,5]{2,1,0:T(1,128)S(1)}, u32[]{:S(2)}, u32[]{:S(2)}) async-start(s32[8,1,5]{2,1,0:T(1,128)} %bitcast.25), calls=%async_computation | async-start | bytes 8192 | tf_op jit(solution)/shard_map/all_to_all | solution.py:73
  25.8 2.2 copy-start.3
  37.7 415.7 %all-to-all-start.1 = ((bf16[8,5,64,2048]{3,2,1,0:T(8,128)(2,1)}), bf16[8,5,64,2048]{3,2,1,0:T(8,128)(2,1)}, u32[]{:S(2)}, u32[]{:S(2)}) async-start(bf16[8,5,64,2048]{3,2,1,0:T(8,128)(2,1)} %bitcast.117), calls=%async_computation.1 | async-start | bytes 20971520 | tf_op jit(solution)/shard_map/all_to_all | solution.py:78
  43.8 276.6 %all-reduce.3.cloned.1.call-start = ((), (), s32[]{:S(2)}) async-start(), calls=%async_computation.3 | async-start | bytes 1572864 | tf_op jit(solution)/shard_map/psum | solution.py:14
  45.9 374.8 %all-gather.5.cloned.1.call-start = ((), (), s32[]{:S(2)}) async-start(), calls=%async_computation.2 | async-start | bytes 4718592 | tf_op jit(solution)/shard_map/all_gather | solution.py:31
  322.6 5.3 copy-start.4
  325.3 2.6 copy-start.1
  333.9 15.5 %collective-permute-start = (bf16[64,2048]{1,0:T(8,128)(2,1)}, bf16[64,2048]{1,0:T(8,128)(2,1)S(1)}, u32[]{:S(2)}, u32[]{:S(2)}) collective-permute-start(bf16[64,2048]{1,0:T(8,128)(2,1)} %get-tuple-element.193), channel_id=1, source_target_pairs={{0,1},{1,2},{2,3},{3,4},{4,5},{5,6},{6,7},{8,9},{9,10},{10,11},{11... | collective-permute-start | bytes 786440 | tf_op jit(solution)/shard_map/ppermute | solution.py:24
  336.4 15.1 %collective-permute-start.1 = (bf16[64,2048]{1,0:T(8,128)(2,1)}, bf16[64,2048]{1,0:T(8,128)(2,1)S(1)}, u32[]{:S(2)}, u32[]{:S(2)}) collective-permute-start(bf16[64,2048]{1,0:T(8,128)(2,1)} %get-tuple-element.194), channel_id=1, source_target_pairs={{1,0},{2,1},{3,2},{4,3},{5,4},{6,5},{7,6},{9,8},{10,9},{11,10},{12... | collective-permute-start | bytes 786440 | tf_op jit(solution)/shard_map/ppermute | solution.py:25
  343.5 11.3 %copy-start.2 = (f32[16,768,128]{2,1,0:T(8,128)S(1)}, f32[16,768,128]{2,1,0:T(8,128)}, u32[]{:S(2)}) copy-start(f32[16,768,128]{2,1,0:T(8,128)} %copy-done.1) | copy-start | bytes 18874372
  462.8 166.2 %copy-start.5 = (bf16[64,1024]{1,0:T(8,128)(2,1)S(1)}, bf16[64,1024]{1,0:T(8,128)(2,1)}, u32[]{:S(2)}) copy-start(bf16[64,1024]{1,0:T(8,128)(2,1)} %slice.101) | copy-start | bytes 393220
  462.8 166.2 %copy-start.6 = (bf16[64,1024]{1,0:T(8,128)(2,1)S(1)}, bf16[64,1024]{1,0:T(8,128)(2,1)}, u32[]{:S(2)}) copy-start(bf16[64,1024]{1,0:T(8,128)(2,1)} %slice.110) | copy-start | bytes 393220
Sparse Core Ops, SparseCore 0:
  48.1 272.2 all-reduce.2
  332.1 83.8 all-gather.4
where the time goes:
time: 643 us; the launch traced here: 640 us
  waiting for transfers between devices  272 us (42%)
  local copies, waits for them, and re-layouts  186 us (29%)
  blocking collectives  63.9 us (10%)
  matrix products  61.6 us (10%)
  other arithmetic  22.3 us (3%)
  starting transfers between devices  17.4 us (3%)
  between operations  13.7 us (2%)
    psum x1, waiting for transfers between devices, from_root(): return lax.psum(jnp.where(mine, shard, jnp.zeros_like(shard)), axis)  264 us
    all_gather x2, blocking collectives, combined_all(): pieces = jax.tree.map(lambda part: lax.all_gather(part, axis), value)  63.9 us
    slice x6, local copies, waits for them, and re-layouts, attend(): gathered[:, :, :width].reshape(group_size, 8 * BLOCK, HEADS, head_dim)  36.9 us
    while x12, local copies, waits for them, and re-layouts  28.4 us
    sub x3, matrix products, attend(): exponent = jnp.exp(scores - row_top)  23.5 us
    dot_general x3, matrix products, attend(): jnp.einsum('ghqk,gkhd->gqhd', weights, group_values, preferred_element_ty...  20.9 us
    slice x3, local copies, waits for them, and re-layouts, attend(): gathered[:, :, width:].reshape(group_size, 8 * BLOCK, HEADS, head_dim)  18.6 us
    add x7, other arithmetic, combine_partial(): partial_a[2] * factor_a[..., None] + partial_b[2] * factor_b[..., None]  13.2 us
  transfers between devices with their start and end apart: 6, of which 3 were waited for; matrix products, arithmetic and copies ran while one was open for 12% of the time, Pallas kernels for 0%

commit v1 on v0

v1 whole, which is shorter than its diff:
```python
import functools

import jax
import jax.numpy as jnp
from jax import lax
from jax.experimental import pallas as pl
from jax.experimental.pallas import tpu as pltpu
from jax.sharding import PartitionSpec as P

HEADS = 16
BLOCK = 64
HD = 64
MESH = pl.DeviceIdType.MESH


def request_slots(owners, n_dev, capacity):
    flat_owner = owners.reshape(-1)
    onehot = (flat_owner[:, None] == jnp.arange(n_dev, dtype=jnp.int32)[None, :]).astype(jnp.int32)
    before = jnp.cumsum(onehot, axis=0) - onehot
    rank_of = jnp.sum(before * onehot, axis=1)
    return flat_owner * capacity + rank_of


def greet_all(me, n):
    barrier = pltpu.get_barrier_semaphore()
    for d in range(1, n):
        pl.semaphore_signal(
            barrier, inc=1, device_id={"ctx": lax.rem(me + d, n)}, device_id_type=MESH
        )
    pl.semaphore_wait(barrier, n - 1)


def remote(src, dst, send, recv, target):
    return pltpu.make_async_remote_copy(
        src_ref=src,
        dst_ref=dst,
        send_sem=send,
        recv_sem=recv,
        device_id={"ctx": target},
        device_id_type=MESH,
    )


def rim_kernel(n, rows, x_ref, o_ref, own_sem, edge_sem, send_sem, halo_send, recv_sem):
    me = lax.axis_index("ctx")
    first = x_ref.at[pl.ds(0, BLOCK)]
    last = x_ref.at[pl.ds(rows - BLOCK, BLOCK)]
    prev = o_ref.at[pl.ds(0, BLOCK)]
    after = o_ref.at[pl.ds(rows + BLOCK, BLOCK)]
    glob0 = o_ref.at[pl.ds(rows + 2 * BLOCK, BLOCK)]
    glob1 = o_ref.at[pl.ds(rows + 3 * BLOCK, BLOCK)]
    own = pltpu.make_async_copy(x_ref, o_ref.at[pl.ds(BLOCK, rows)], own_sem)
    own.start()
    greet_all(me, n)
    up, down = lax.rem(me + 1, n), lax.rem(me + n - 1, n)
    to_next = remote(last, prev, halo_send.at[0], recv_sem.at[0], up)
    to_prev = remote(first, after, halo_send.at[1], recv_sem.at[1], down)

    @pl.when(me < n - 1)
    def _():
        to_next.start()

    @pl.when(me > 0)
    def _():
        to_prev.start()

    @pl.when(me == 0)
    def _():
        sends = [remote(first, glob0, send_sem.at[d], recv_sem.at[2], d) for d in range(1, n)]
        for c in sends:
            c.start()
        mine = [
            pltpu.make_async_copy(first, glob0, edge_sem.at[0]),
            pltpu.make_async_copy(first, prev, edge_sem.at[1]),
        ]
        for c in mine:
            c.start()
        for c in mine:
            c.wait()
        for c in sends:
            c.wait_send()

    @pl.when(me == n - 1)
    def _():
        sends = [remote(last, glob1, send_sem.at[d], recv_sem.at[3], d) for d in range(n - 1)]
        for c in sends:
            c.start()
        mine = [
            pltpu.make_async_copy(last, glob1, edge_sem.at[0]),
            pltpu.make_async_copy(last, after, edge_sem.at[1]),
        ]
        for c in mine:
            c.start()
        for c in mine:
            c.wait()
        for c in sends:
            c.wait_send()

    @pl.when(me > 0)
    def _():
        to_prev.wait_send()
        to_next.wait_recv()
        remote(first, glob0, send_sem.at[0], recv_sem.at[2], up).wait_recv()

    @pl.when(me < n - 1)
    def _():
        to_next.wait_send()
        to_prev.wait_recv()
        remote(last, glob1, send_sem.at[0], recv_sem.at[3], up).wait_recv()

    own.wait()


def partial_kernel(rows, width, p_ref, o_ref, lse_ref):
    q_rows = 2 * BLOCK
    row_head = lax.broadcasted_iota(jnp.int32, (2 * q_rows, 128), 0) // q_rows
    col_head = lax.broadcasted_iota(jnp.int32, (2 * q_rows, 128), 1) // HD
    diag = row_head == col_head
    low = lax.broadcasted_iota(jnp.int32, (q_rows, 128), 1) < HD
    for g in range(HEADS // 2):
        c = g * 128
        q = p_ref[pl.ds(rows + 2 * BLOCK, q_rows), pl.ds(c, 128)] * jnp.bfloat16(0.125)
        qd = jnp.where(diag, jnp.concatenate([q, q], axis=0), jnp.zeros_like(q[:1]))
        k = p_ref[pl.ds(BLOCK, rows), pl.ds(width + c, 128)]
        v = p_ref[pl.ds(BLOCK, rows), pl.ds(2 * width + c, 128)]
        s = lax.dot_general(k, qd, (((1,), (1,)), ((), ())), preferred_element_type=jnp.float32)
        m = jnp.max(s, axis=0, keepdims=True)
        e = jnp.exp(s - m)
        total = jnp.sum(e, axis=0, keepdims=True)
        w = e * (1.0 / total)
        hi = w.astype(jnp.bfloat16)
        lo = (w - hi.astype(jnp.float32)).astype(jnp.bfloat16)
        dims = (((0,), (0,)), ((), ()))
        out = lax.dot_general(hi, v, dims, preferred_element_type=jnp.float32)
        out += lax.dot_general(lo, v, dims, preferred_element_type=jnp.float32)
        mixed = jnp.where(low, out[:q_rows], out[q_rows:]).astype(o_ref.dtype)
        o_ref[0, :, pl.ds(c, 128)] = mixed[:BLOCK]
        o_ref[1, :, pl.ds(c, 128)] = mixed[BLOCK:]
        lse_ref[pl.ds(g, 1), :] = m + jnp.log(total)


def collect_kernel(n, part_ref, lse_ref, o_ref, ol_ref, sends, lsends, recvs, lrecvs, locals_):
    me = lax.axis_index("ctx")
    greet_all(me, n)
    for t, target in enumerate((0, n - 1)):
        a = remote(part_ref.at[t], o_ref.at[me], sends.at[t], recvs.at[me], target)
        b = remote(lse_ref, ol_ref.at[me], lsends.at[t], lrecvs.at[me], target)

        @pl.when(me != target)
        def _():
            a.start()
            b.start()

        @pl.when(me == target)
        def _():
            c = pltpu.make_async_copy(part_ref.at[t], o_ref.at[target], locals_.at[0])
            d = pltpu.make_async_copy(lse_ref, ol_ref.at[target], locals_.at[1])
            c.start()
            d.start()
            c.wait()
            d.wait()

    for t, target in enumerate((0, n - 1)):

        @pl.when(me != target)
        def _():
            remote(part_ref.at[t], o_ref.at[me], sends.at[t], recvs.at[me], target).wait_send()
            remote(lse_ref, ol_ref.at[me], lsends.at[t], lrecvs.at[me], target).wait_send()

        @pl.when(me == target)
        def _():
            for src in range(n):
                if src != target:
                    remote(
                        part_ref.at[t], o_ref.at[src], sends.at[t], recvs.at[src], src
                    ).wait_recv()
                    remote(
                        lse_ref, ol_ref.at[src], lsends.at[t], lrecvs.at[src], src
                    ).wait_recv()


def attend_kernel(
    n_local, width, slots, usable, use_glob, p_ref, r0, r1, r2, glob_ref, o_ref
):
    i = pl.program_id(0)
    row_head = lax.broadcasted_iota(jnp.int32, (256, 256), 0) // HD
    col_head = lax.broadcasted_iota(jnp.int32, (256, 256), 1) // HD
    diag = row_head == col_head
    lane_head = lax.broadcasted_iota(jnp.int32, (BLOCK, 256), 1) // HD
    near = pl.ds(pl.multiple_of(i * BLOCK, BLOCK), 3 * BLOCK)
    mine = pl.ds(pl.multiple_of(i * BLOCK + BLOCK, BLOCK), BLOCK)
    ends = pl.ds((n_local + 2) * BLOCK, 2 * BLOCK)
    live = [usable[i * 8 + b] > 0 for b in range(8)]
    for g in range(HEADS // 4):
        c = g * 256
        q = p_ref[mine, pl.ds(c, 256)] * jnp.bfloat16(0.125)
        qd = jnp.where(diag, jnp.concatenate([q] * 4, axis=0), jnp.zeros_like(q[:1]))

        def rows_of(base):
            return jnp.concatenate(
                [p_ref[near, pl.ds((1 + base) * width + c, 256)], p_ref[ends, pl.ds((1 + base) * width + c, 256)]]
                + [r[:, pl.ds(base * width + c, 256)] for r in (r0, r1, r2)],
                axis=0,
            )

        s = lax.dot_general(
            rows_of(0), qd, (((1,), (1,)), ((), ())), preferred_element_type=jnp.float32
        )
        s = jnp.concatenate(
            [
                jnp.where(live[b], s[b * BLOCK : (b + 1) * BLOCK], -jnp.inf)
                if b not in (1, 3, 4)
                else s[b * BLOCK : (b + 1) * BLOCK]
                for b in range(8)
            ],
            axis=0,
        )
        m = jnp.max(s, axis=0, keepdims=True)
        e = jnp.exp(s - m)
        w = (e * (1.0 / jnp.sum(e, axis=0, keepdims=True))).astype(jnp.bfloat16)
        out = lax.dot_general(
            w, rows_of(1), (((0,), (0,)), ((), ())), preferred_element_type=jnp.float32
        )
        ctx = out[:BLOCK]
        for h in range(1, 4):
            ctx = jnp.where(lane_head == h, out[h * BLOCK : (h + 1) * BLOCK], ctx)
        ctx = jnp.where(use_glob[i] > 0, glob_ref[:, pl.ds(c, 256)], ctx)
        o_ref[:, pl.ds(c, 256)] = ctx.astype(o_ref.dtype)


def per_device(inputs, qkv_weight, out_weight, rand_owner, rand_local):
    rows, width = inputs.shape
    n_local = rows // BLOCK
    n = lax.axis_size("ctx")
    me = lax.axis_index("ctx")
    capacity = max(2, (3 * n_local + n - 1) // n)
    any_spec = pl.BlockSpec(memory_space=pl.ANY)
    dma = pltpu.SemaphoreType.DMA

    slot_ids = request_slots(rand_owner, n, capacity)
    table = jnp.zeros((n * capacity,), jnp.int32).at[slot_ids].set(rand_local.reshape(-1))
    asked_for = lax.all_to_all(
        table.reshape(n, capacity), "ctx", split_axis=0, concat_axis=0, tiled=True
    )
    outgoing = inputs.reshape(n_local, BLOCK, width)[asked_for.reshape(-1)]
    outgoing = outgoing.reshape(n, capacity * BLOCK, width)
    arrived = lax.all_to_all(outgoing, "ctx", split_axis=0, concat_axis=0, tiled=True)

    rimmed = pl.pallas_call(
        functools.partial(rim_kernel, n, rows),
        out_shape=jax.ShapeDtypeStruct((rows + 4 * BLOCK, width), inputs.dtype),
        in_specs=[any_spec],
        out_specs=any_spec,
        scratch_shapes=[dma, dma((2,)), dma((n,)), dma((2,)), dma((4,))],
        compiler_params=pltpu.CompilerParams(collective_id=0, has_side_effects=True),
        name="rim",
    )(inputs)
    near = jnp.dot(rimmed, qkv_weight, preferred_element_type=jnp.float32).astype(jnp.bfloat16)

    part, lse = pl.pallas_call(
        functools.partial(partial_kernel, rows, width),
        out_shape=(
            jax.ShapeDtypeStruct((2, BLOCK, width), jnp.bfloat16),
            jax.ShapeDtypeStruct((HEADS // 2, 4 * BLOCK), jnp.float32),
        ),
        compiler_params=pltpu.CompilerParams(vmem_limit_bytes=40 * 1024 * 1024),
        cost_estimate=pl.CostEstimate(flops=10**9, bytes_accessed=7 * 10**6, transcendentals=10**6),
        name="partial",
    )(near)
    parts, lses = pl.pallas_call(
        functools.partial(collect_kernel, n),
        out_shape=(
            jax.ShapeDtypeStruct((n, BLOCK, width), jnp.bfloat16),
            jax.ShapeDtypeStruct((n, HEADS // 2, 4 * BLOCK), jnp.float32),
        ),
        in_specs=[any_spec] * 2,
        out_specs=(any_spec, any_spec),
        scratch_shapes=[dma((2,)), dma((2,)), dma((n,)), dma((n,)), dma((2,))],
        compiler_params=pltpu.CompilerParams(collective_id=1, has_side_effects=True),
        name="collect",
    )(part, lse)
    is_first, is_last = me == 0, me == n - 1
    gather_here = is_first | is_last
    parts = jnp.where(gather_here, parts, 0)
    lses = jnp.where(gather_here, lses, 0.0).reshape(n, HEADS, 2, BLOCK)
    lses = jnp.where(is_first, lses[:, :, 0], lses[:, :, 1])
    share = jax.nn.softmax(lses, axis=0).transpose(0, 2, 1)
    glob = jnp.sum(parts.astype(jnp.float32) * jnp.repeat(share, HD, axis=2), axis=0)

    n_blocks = n_local * n
    block_ids = me * n_local + jnp.arange(n_local, dtype=jnp.int32)
    rand_ids = rand_owner * n_local + rand_local
    window_ids = jnp.stack([block_ids - 1, block_ids, block_ids + 1], axis=1)
    global_ids = jnp.broadcast_to(jnp.array([0, n_blocks - 1], jnp.int32), (n_local, 2))
    fixed_ids = jnp.concatenate([window_ids, global_ids], axis=1)
    window_ok = jnp.stack(
        [block_ids - 1 >= 1, block_ids >= 0, block_ids + 1 < n_blocks - 1], axis=1
    )
    rand_ok = jnp.all(rand_ids[:, :, None] != fixed_ids[:, None, :], axis=2)
    usable = jnp.concatenate([window_ok, jnp.ones((n_local, 2), bool), rand_ok], axis=1)
    use_glob = ((block_ids == 0) | (block_ids == n_blocks - 1)).astype(jnp.int32)

    far = jnp.dot(
        arrived.reshape(n * capacity * BLOCK, width),
        qkv_weight[:, width:],
        preferred_element_type=jnp.float32,
    ).astype(jnp.bfloat16)

    def pick(s):
        return pl.BlockSpec((BLOCK, 2 * width), lambda i, slots, *_: (slots[i * 3 + s], 0))

    context = pl.pallas_call(
        functools.partial(attend_kernel, n_local, width),
        out_shape=jax.ShapeDtypeStruct((rows, width), jnp.bfloat16),
        grid_spec=pltpu.PrefetchScalarGridSpec(
            num_scalar_prefetch=3,
            grid=(n_local,),
            in_specs=[
                pl.BlockSpec((rows + 4 * BLOCK, 3 * width), lambda i, *_: (0, 0)),
                pick(0),
                pick(1),
                pick(2),
                pl.BlockSpec((BLOCK, width), lambda i, *_: (0, 0)),
            ],
            out_specs=pl.BlockSpec((BLOCK, width), lambda i, *_: (i, 0)),
        ),
        compiler_params=pltpu.CompilerParams(vmem_limit_bytes=40 * 1024 * 1024),
        name="attend",
    )(
        slot_ids,
        usable.astype(jnp.int32).reshape(-1),
        use_glob,
        near,
        far,
        far,
        far,
        glob,
    )
    return jnp.dot(context, out_weight, preferred_element_type=jnp.float32).astype(jnp.bfloat16)


def solution(mesh):
    in_specs = (P(("seq", "ctx"), None), P(), P(), P(("seq", "ctx"), None), P(("seq", "ctx"), None))
    out_specs = P(("seq", "ctx"), None)
    return jax.shard_map(
        per_device, mesh=mesh, in_specs=in_specs, out_specs=out_specs, check_vma=False
    )
```

time: 643 us -> 241 us (0.37)
  waiting for transfers between devices: 272 us -> 0.01 us
  Pallas kernels: 0 us -> 164 us
  local copies, waits for them, and re-layouts: 186 us -> 24.2 us
  blocking collectives: 63.9 us -> 13.5 us
  matrix products: 61.6 us -> 29.4 us
  other arithmetic: 22.3 us -> 4.86 us
  between operations: 13.7 us -> 0.21 us
  starting transfers between devices: 17.4 us -> 4.65 us
    psum x1 -> x0, waiting for transfers between devices: 264 us -> none  [from_root(): return lax.psum(jnp.where(mine, shard, jnp.zeros_like(shard)), axis)]
    pallas_call x0 -> x4, Pallas kernels: none -> 164 us  [the longest x1 101 us: per_device(): pl.pallas_call(functools.partial(rim_kernel, n, rows), out_shape=jax.Shap...]
    slice x29 -> x0, local copies, waits for them, and re-layouts: 79.8 us -> none  [the longest x6 36.9 us: attend(): gathered[:, :, :width].reshape(group_size, 8 * BLOCK, HEADS, head_dim)]
    all_gather x2 -> x0, blocking collectives: 63.9 us -> none  [combined_all(): pieces = jax.tree.map(lambda part: lax.all_gather(part, axis), value)]
    while x16 -> x0, local copies, waits for them, and re-layouts: 37.7 us -> none
    sub x3 -> x0, matrix products: 23.5 us -> none  [attend(): exponent = jnp.exp(scores - row_top)]
    add x16 -> x2, other arithmetic: 14 us -> 0.01 us  [the longest x1 0.01 us: per_device(): block_ids = me * n_local + jnp.arange(n_local, dtype=jnp.int32)]
    all_to_all x0 -> x1, blocking collectives: none -> 13.5 us  [per_device(): lax.all_to_all(table.reshape(n, capacity), 'ctx', split_axis=0, concat_ax...]
  transfers between devices with their start and end apart: 6 -> 1, of which waited for: 3 -> 0; matrix products, arithmetic and copies ran while one was open for 12% -> 9% of each run, Pallas kernels for 0% -> 59%
where the time goes in v1:
time: 241 us; the launch traced here: 240 us
  Pallas kernels  164 us (68%)
  matrix products  29.4 us (12%)
  local copies, waits for them, and re-layouts  24.2 us (10%)
  blocking collectives  13.5 us (6%)
  other arithmetic  4.86 us (2%)
  starting transfers between devices  4.65 us (2%)
    pallas_call x1, Pallas kernels, per_device(): pl.pallas_call(functools.partial(rim_kernel, n, rows), out_shape=jax.Shap...  101 us
    pallas_call x1, Pallas kernels, per_device(): pl.pallas_call(functools.partial(collect_kernel, n), out_shape=(jax.Shape...  33.7 us
    pallas_call x1, Pallas kernels, per_device(): pl.pallas_call(functools.partial(attend_kernel, n_local, width), out_shap...  22.5 us
    dot_general x1, matrix products, per_device(): jnp.dot(arrived.reshape(n * capacity * BLOCK, width), qkv_weight[:, width...  17 us
    all_to_all x1, blocking collectives, per_device(): lax.all_to_all(table.reshape(n, capacity), 'ctx', split_axis=0, concat_ax...  13.5 us
    dot_general x1, matrix products, per_device(): jnp.dot(rimmed, qkv_weight, preferred_element_type=jnp.float32)  9.42 us
    unnamed x14, local copies, waits for them, and re-layouts  8.34 us
    pallas_call x1, Pallas kernels, per_device(): pl.pallas_call(functools.partial(partial_kernel, rows, width), out_shape=...  6.39 us
  transfers between devices with their start and end apart: 1, of which 0 were waited for; matrix products, arithmetic and copies ran while one was open for 9% of the time, Pallas kernels for 59%

profile of v1, /device:TPU:0, one launch (start us, length us, event | category | flops | bytes accessed | tf_op | source)
XLA Modules:
  0.0 240.5 jit_solution(2707219683617149938)
XLA Ops:
  0.0 0.0 copy-start
  0.0 0.9 copy.23
  0.9 0.7 broadcast_multiply_fusion
  1.6 0.8 copy.26
  2.4 0.1 copy.25
  2.5 0.1 mul.43
  2.6 0.1 reshape.123
  2.7 0.1 reshape.144
  2.8 0.1 fusion.2
  2.8 0.1 reduce_window_sum.11
  2.9 0.2 select_reduce_fusion
  3.1 0.7 scatter_custom_fusion
  3.8 0.1 all_to_all.9
  3.9 13.5 %all_to_all.14 = s32[8,1,5]{2,1,0:T(1,128)S(1)} all-to-all(s32[8,1,5]{2,1,0:T(1,128)S(1)} %bitcast.27), channel_id=1, replica_groups=mesh['seq'=4,'ctx'=8] {'ctx'}, dimensions={0} | all-to-all | bytes 320 | tf_op jit(solution)/shard_map/all_to_all | solution.py:242
  17.4 0.5 broadcast.175
  17.9 0.7 reduce.4
  18.6 0.1 reshape.126
  18.6 6.0 %gather_fusion = bf16[40,64,1024]{2,1,0:T(8,128)(2,1)} fusion(bf16[12,64,1024]{2,1,0:T(8,128)(2,1)} %bitcast.23, s32[1024]{0:T(1024)S(1)} %pad_clamp_fusion), kind=kCustom, calls=%fused_computation | custom fusion | bytes 10485920 | tf_op jit(solution)/shard_map/gather | solution.py:245
  24.7 4.7 %all-to-all-start.1 = ((bf16[8,320,1024]{2,1,0:T(8,128)(2,1)}), bf16[8,320,1024]{2,1,0:T(8,128)(2,1)}, u32[]{:S(2)}, u32[]{:S(2)}) async-start(bf16[8,320,1024]{2,1,0:T(8,128)(2,1)} %bitcast.24), calls=%async_computation.1 | async-start | bytes 10485760 | tf_op jit(solution)/shard_map/all_to_all | solution.py:247
  29.3 101.1 %rim.1 = bf16[1024,1024]{1,0:T(8,128)(2,1)} custom-call(bf16[768,1024]{1,0:T(8,128)(2,1)} %x_ref.1), custom_call_target="tpu_custom_call" | custom-call | tf_op jit(solution)/shard_map/rim/pallas_call | solution.py:249
  130.4 0.1 pad.3.clone
  130.5 0.1 add_add_fusion
  130.7 0.1 copy.24
  130.8 0.1 reshape.131.usable
  130.9 9.4 %convolution_convert_fusion.1.p_ref = bf16[1024,3072]{1,0:T(8,128)(2,1)S(1)} fusion(bf16[1024,1024]{1,0:T(8,128)(2,1)} %rim.1, bf16[1024,3072]{1,0:T(8,128)(2,1)} %param.7), kind=kOutput, calls=%fused_computation.3 | convolution fusion | flops 6445596672 | bytes 14680064 | tf_op jit(solution)/shard_map/dot_general | solution.py:258
  140.3 6.4 %partial.1 = (bf16[2,64,1024]{2,1,0:T(8,128)(2,1)S(1)}, f32[8,256]{1,0:T(8,128)S(1)}) custom-call(bf16[1024,3072]{1,0:T(8,128)(2,1)S(1)} %convolution_convert_fusion.1.p_ref), custom_call_target="tpu_custom_call" | custom-call | flops 1000000000 | bytes 7000000 | tf_op jit(solution)/shard_map/partial/pallas_call | solution.py:260
  146.7 0.0 copy-start.1
  146.7 2.6 %copy-done.1 = bf16[1024,3072]{1,0:T(8,128)(2,1)} copy-done((bf16[1024,3072]{1,0:T(8,128)(2,1)}, bf16[1024,3072]{1,0:T(8,128)(2,1)S(1)}, u32[]{:S(2)}) %copy-start.1) | copy-done | bytes 6291480
  149.3 0.0 copy-start.3
  149.3 0.7 copy-done.3
  150.0 0.0 copy-start.4
  150.0 0.6 copy-done.4
  150.6 33.7 %collect.1 = (bf16[8,64,1024]{2,1,0:T(8,128)(2,1)}, f32[8,8,256]{2,1,0:T(8,128)}) custom-call(bf16[2,64,1024]{2,1,0:T(8,128)(2,1)} %copy-done.3, f32[8,256]{1,0:T(8,128)} %copy-done.4), custom_call_target="tpu_custom_call" | custom-call | tf_op jit(solution)/shard_map/collect/pallas_call | solution.py:270
  184.3 0.9 broadcast_select_fusion.1
  185.1 0.1 reshape.129
  185.2 0.1 fusion.7
  185.4 0.1 copy.28
  185.6 2.6 %broadcast_in_dim.24 = f32[8,64,16,64]{3,2,1,0:T(8,128)} broadcast(f32[8,64,16]{2,1,0:T(8,128)S(1)} %copy.28), dimensions={0,1,2} | broadcast | bytes 2129920 | tf_op jit(solution)/shard_map/broadcast_in_dim | solution.py:288
  188.2 0.0 copy-start.5
  188.2 5.0 %reshape.130 = f32[8,64,1024]{2,1,0:T(8,128)} reshape(f32[8,64,16,64]{3,2,1,0:T(8,128)} %broadcast_in_dim.24) | data formatting | bytes 4194304 | tf_op jit(solution)/shard_map/reshape | solution.py:288
  193.2 0.0 copy-done.5
  193.2 2.0 multiply_reduce_fusion.glob_ref
  195.2 0.0 all-to-all-done.1
  195.2 17.0 %convolution_convert_fusion.r0.r1.r2 = bf16[2560,2048]{1,0:T(8,128)(2,1)} fusion(bf16[2560,1024]{1,0:T(8,128)(2,1)} %bitcast.6, bf16[1024,3072]{1,0:T(8,128)(2,1)} %param.7), kind=kOutput, calls=%fused_computation.2 | convolution fusion | flops 10742661120 | bytes 19922944 | tf_op jit(solution)/shard_map/dot_general | solution.py:303
  212.2 2.8 %copy-done.2 = bf16[1024,3072]{1,0:T(8,128)(2,1)S(1)} copy-done((bf16[1024,3072]{1,0:T(8,128)(2,1)S(1)}, bf16[1024,3072]{1,0:T(8,128)(2,1)}, u32[]{:S(2)}) %copy-start.2) | copy-done | bytes 6291480
  215.0 22.5 %attend.1 = bf16[768,1024]{1,0:T(8,128)(2,1)S(1)} custom-call(s32[36]{0:T(128)S(1)} %multiply_add_fusion.1.slots, s32[96]{0:T(128)S(1)} %reshape.131.usable, s32[12]{0:T(128)S(1)} %or_convert_fusion.use_glob, bf16[1024,3072]{1,0:T(8,128)(2,1)S(1)} %copy-done.2, bf16[2560,2048]{1,0:T(8,128)(2,1)} %convolution_convert_fusion.r0.r1.r2, ...), custom_call_target="tpu_custom_call" | custom-call | tf_op jit(solution)/shard_map/attend/pallas_call | solution.py:312
  237.5 0.0 copy-done
  237.5 2.9 %convolution_convert_fusion.2 = bf16[768,1024]{1,0:T(8,128)(2,1)} fusion(bf16[768,1024]{1,0:T(8,128)(2,1)S(1)} %attend.1, bf16[1024,1024]{1,0:T(8,128)(2,1)S(1)} %copy-done), kind=kOutput, calls=%fused_computation.6 | convolution fusion | flops 1611399168 | bytes 5242880 | tf_op jit(solution)/shard_map/dot_general | solution.py:339
  (17 shorter events, 0.2 us)
Async XLA Ops:
  0.0 237.5 %copy-start = (bf16[1024,1024]{1,0:T(8,128)(2,1)S(1)}, bf16[1024,1024]{1,0:T(8,128)(2,1)}, u32[]{:S(2)}) copy-start(bf16[1024,1024]{1,0:T(8,128)(2,1)} %param.8) | copy-start | bytes 6291460
  24.7 170.5 %all-to-all-start.1 = ((bf16[8,320,1024]{2,1,0:T(8,128)(2,1)}), bf16[8,320,1024]{2,1,0:T(8,128)(2,1)}, u32[]{:S(2)}, u32[]{:S(2)}) async-start(bf16[8,320,1024]{2,1,0:T(8,128)(2,1)} %bitcast.24), calls=%async_computation.1 | async-start | bytes 10485760 | tf_op jit(solution)/shard_map/all_to_all | solution.py:247
  146.7 2.6 %copy-start.1 = (bf16[1024,3072]{1,0:T(8,128)(2,1)}, bf16[1024,3072]{1,0:T(8,128)(2,1)S(1)}, u32[]{:S(2)}) copy-start(bf16[1024,3072]{1,0:T(8,128)(2,1)S(1)} %convolution_convert_fusion.1.p_ref) | copy-start | bytes 18874372
  149.3 0.7 copy-start.3
  150.0 0.6 copy-start.4
  188.2 5.0 %copy-start.5 = (bf16[8,64,1024]{2,1,0:T(8,128)(2,1)S(1)}, bf16[8,64,1024]{2,1,0:T(8,128)(2,1)}, u32[]{:S(2)}) copy-start(bf16[8,64,1024]{2,1,0:T(8,128)(2,1)} %get-tuple-element.11) | copy-start | bytes 3145732
  212.2 2.8 %copy-start.2 = (bf16[1024,3072]{1,0:T(8,128)(2,1)S(1)}, bf16[1024,3072]{1,0:T(8,128)(2,1)}, u32[]{:S(2)}) copy-start(bf16[1024,3072]{1,0:T(8,128)(2,1)} %copy-done.1) | copy-start | bytes 18874372

commit v2 on v1

--- a/solution.py
+++ b/solution.py
@@ -41,7 +41,9 @@
     )
 
 
-def rim_kernel(n, rows, x_ref, o_ref, own_sem, edge_sem, send_sem, halo_send, recv_sem):
+def rim_kernel(
+    n, rows, x_ref, t_ref, o_ref, a_ref, own_sem, edge_sem, send_sem, halo_send, recv_sem, asks, asked
+):
     me = lax.axis_index("ctx")
     first = x_ref.at[pl.ds(0, BLOCK)]
     last = x_ref.at[pl.ds(rows - BLOCK, BLOCK)]
@@ -51,7 +53,14 @@
     glob1 = o_ref.at[pl.ds(rows + 3 * BLOCK, BLOCK)]
     own = pltpu.make_async_copy(x_ref, o_ref.at[pl.ds(BLOCK, rows)], own_sem)
     own.start()
+    keep = pltpu.make_async_copy(t_ref.at[me], a_ref.at[me], asks.at[0])
+    keep.start()
     greet_all(me, n)
+    requests = []
+    for d in range(1, n):
+        to = lax.rem(me + d, n)
+        requests.append(remote(t_ref.at[to], a_ref.at[me], asks.at[d], asked.at[d], to))
+        requests[-1].start()
     up, down = lax.rem(me + 1, n), lax.rem(me + n - 1, n)
     to_next = remote(last, prev, halo_send.at[0], recv_sem.at[0], up)
     to_prev = remote(first, after, halo_send.at[1], recv_sem.at[1], down)
@@ -108,6 +117,11 @@
         to_prev.wait_recv()
         remote(last, glob1, send_sem.at[0], recv_sem.at[3], up).wait_recv()
 
+    for d in range(1, n):
+        requests[d - 1].wait_send()
+        source = lax.rem(me + n - d, n)
+        remote(t_ref.at[source], a_ref.at[source], asks.at[d], asked.at[d], source).wait_recv()
+    keep.wait()
     own.wait()
 
 
@@ -180,7 +194,7 @@
 
 
 def attend_kernel(
-    n_local, width, slots, usable, use_glob, p_ref, r0, r1, r2, glob_ref, o_ref
+    n_local, width, sa, sb, late, usable, use_glob, p_ref, a0, a1, a2, b0, b1, b2, glob_ref, o_ref
 ):
     i = pl.program_id(0)
     row_head = lax.broadcasted_iota(jnp.int32, (256, 256), 0) // HD
@@ -190,6 +204,7 @@
     near = pl.ds(pl.multiple_of(i * BLOCK, BLOCK), 3 * BLOCK)
     mine = pl.ds(pl.multiple_of(i * BLOCK + BLOCK, BLOCK), BLOCK)
     ends = pl.ds((n_local + 2) * BLOCK, 2 * BLOCK)
+    is_late = [late[i * 3 + s] > 0 for s in range(3)]
     live = [usable[i * 8 + b] > 0 for b in range(8)]
     for g in range(HEADS // 4):
         c = g * 256
@@ -199,7 +214,10 @@
         def rows_of(base):
             return jnp.concatenate(
                 [p_ref[near, pl.ds((1 + base) * width + c, 256)], p_ref[ends, pl.ds((1 + base) * width + c, 256)]]
-                + [r[:, pl.ds(base * width + c, 256)] for r in (r0, r1, r2)],
+                + [
+                    jnp.where(w, b[:, pl.ds(base * width + c, 256)], a[:, pl.ds(base * width + c, 256)])
+                    for w, a, b in zip(is_late, (a0, a1, a2), (b0, b1, b2))
+                ],
                 axis=0,
             )
 
@@ -239,22 +257,32 @@
 
     slot_ids = request_slots(rand_owner, n, capacity)
     table = jnp.zeros((n * capacity,), jnp.int32).at[slot_ids].set(rand_local.reshape(-1))
-    asked_for = lax.all_to_all(
-        table.reshape(n, capacity), "ctx", split_axis=0, concat_axis=0, tiled=True
-    )
-    outgoing = inputs.reshape(n_local, BLOCK, width)[asked_for.reshape(-1)]
-    outgoing = outgoing.reshape(n, capacity * BLOCK, width)
-    arrived = lax.all_to_all(outgoing, "ctx", split_axis=0, concat_axis=0, tiled=True)
-
-    rimmed = pl.pallas_call(
+    table = jnp.pad(table.reshape(n, 1, capacity), ((0, 0), (0, 7), (0, 128 - capacity)))
+
+    rimmed, asked_for = pl.pallas_call(
         functools.partial(rim_kernel, n, rows),
-        out_shape=jax.ShapeDtypeStruct((rows + 4 * BLOCK, width), inputs.dtype),
-        in_specs=[any_spec],
-        out_specs=any_spec,
-        scratch_shapes=[dma, dma((2,)), dma((n,)), dma((2,)), dma((4,))],
+        out_shape=(
+            jax.ShapeDtypeStruct((rows + 4 * BLOCK, width), inputs.dtype),
+            jax.ShapeDtypeStruct(table.shape, table.dtype),
+        ),
+        in_specs=[any_spec] * 2,
+        out_specs=(any_spec, any_spec),
+        scratch_shapes=[dma, dma((2,)), dma((n,)), dma((2,)), dma((4,)), dma((n,)), dma((n,))],
         compiler_params=pltpu.CompilerParams(collective_id=0, has_side_effects=True),
         name="rim",
-    )(inputs)
+    )(inputs, table)
+    asked_for = asked_for[:, 0, :capacity]
+    head = capacity - 1
+    blocks = inputs.reshape(n_local, BLOCK, width)
+
+    def sent(picked):
+        return blocks[picked.reshape(-1)].reshape(n, -1, width)
+
+    def exchange(outgoing):
+        return lax.all_to_all(outgoing, "ctx", split_axis=0, concat_axis=0, tiled=True)
+
+    outgoing_b = sent(asked_for[:, head:])
+    arrived_a = exchange(sent(asked_for[:, :head]))
     near = jnp.dot(rimmed, qkv_weight, preferred_element_type=jnp.float32).astype(jnp.bfloat16)
 
     part, lse = pl.pallas_call(
@@ -279,6 +307,8 @@
         compiler_params=pltpu.CompilerParams(collective_id=1, has_side_effects=True),
         name="collect",
     )(part, lse)
+    outgoing_b, parts = lax.optimization_barrier((outgoing_b, parts))
+    arrived_b = exchange(outgoing_b)
     is_first, is_last = me == 0, me == n - 1
     gather_here = is_first | is_last
     parts = jnp.where(gather_here, parts, 0)
@@ -300,26 +330,38 @@
     usable = jnp.concatenate([window_ok, jnp.ones((n_local, 2), bool), rand_ok], axis=1)
     use_glob = ((block_ids == 0) | (block_ids == n_blocks - 1)).astype(jnp.int32)
 
-    far = jnp.dot(
-        arrived.reshape(n * capacity * BLOCK, width),
-        qkv_weight[:, width:],
-        preferred_element_type=jnp.float32,
-    ).astype(jnp.bfloat16)
-
-    def pick(s):
-        return pl.BlockSpec((BLOCK, 2 * width), lambda i, slots, *_: (slots[i * 3 + s], 0))
+    kv_weight = qkv_weight[:, width:]
+
+    def project(rows_in):
+        return jnp.dot(
+            rows_in.reshape(-1, width), kv_weight, preferred_element_type=jnp.float32
+        ).astype(jnp.bfloat16)
+
+    far_a, far_b = project(arrived_a), project(arrived_b)
+    owner, rank = slot_ids // capacity, slot_ids % capacity
+    late = (rank == head).astype(jnp.int32)
+    slots_a = jnp.where(late > 0, 0, owner * head + rank)
+    slots_b = jnp.where(late > 0, owner, 0)
+
+    def pick(s, which):
+        return pl.BlockSpec(
+            (BLOCK, 2 * width), lambda i, *refs: (refs[which][i * 3 + s], 0)
+        )
 
     context = pl.pallas_call(
         functools.partial(attend_kernel, n_local, width),
         out_shape=jax.ShapeDtypeStruct((rows, width), jnp.bfloat16),
         grid_spec=pltpu.PrefetchScalarGridSpec(
-            num_scalar_prefetch=3,
+            num_scalar_prefetch=5,
             grid=(n_local,),
             in_specs=[
                 pl.BlockSpec((rows + 4 * BLOCK, 3 * width), lambda i, *_: (0, 0)),
-                pick(0),
-                pick(1),
-                pick(2),
+                pick(0, 0),
+                pick(1, 0),
+                pick(2, 0),
+                pick(0, 1),
+                pick(1, 1),
+                pick(2, 1),
                 pl.BlockSpec((BLOCK, width), lambda i, *_: (0, 0)),
             ],
             out_specs=pl.BlockSpec((BLOCK, width), lambda i, *_: (i, 0)),
@@ -327,13 +369,18 @@
         compiler_params=pltpu.CompilerParams(vmem_limit_bytes=40 * 1024 * 1024),
         name="attend",
     )(
-        slot_ids,
+        slots_a,
+        slots_b,
+        late,
         usable.astype(jnp.int32).reshape(-1),
         use_glob,
         near,
-        far,
-        far,
-        far,
+        far_a,
+        far_a,
+        far_a,
+        far_b,
+        far_b,
+        far_b,
         glob,
     )
     return jnp.dot(context, out_weight, preferred_element_type=jnp.float32).astype(jnp.bfloat16)

time: 241 us -> 272 us (1.13)
  waiting for transfers between devices: 0.01 us -> 98 us
  Pallas kernels: 164 us -> 105 us
  blocking collectives: 13.5 us -> 0 us
  starting transfers between devices: 4.65 us -> 8.47 us
  matrix products: 29.4 us -> 32.3 us
    all_to_all x1 -> x2, waiting for transfers between devices: 0.01 us -> 98 us  [exchange(): lax.all_to_all(outgoing, 'ctx', split_axis=0, concat_axis=0, tiled=True)]
    pallas_call x1, Pallas kernels: 101 us -> 57.1 us  [per_device(): pl.pallas_call(functools.partial(rim_kernel, n, rows), out_shape=(jax.Sha...]
    pallas_call x1, Pallas kernels: 33.7 us -> 19.1 us  [per_device(): pl.pallas_call(functools.partial(collect_kernel, n), out_shape=(jax.Shape...]
    all_to_all x1 -> x0, blocking collectives: 13.5 us -> none  [per_device(): lax.all_to_all(table.reshape(n, capacity), 'ctx', split_axis=0, concat_ax...]
    all_to_all x1 -> x2, starting transfers between devices: 4.65 us -> 8.47 us  [exchange(): lax.all_to_all(outgoing, 'ctx', split_axis=0, concat_axis=0, tiled=True)]
    dot_general x1 -> x2, matrix products: 17 us -> 19.9 us  [project(): jnp.dot(rows_in.reshape(-1, width), kv_weight, preferred_element_type=jnp...]
    unnamed x14 -> x18, local copies, waits for them, and re-layouts: 8.34 us -> 5.71 us
    gather x1 -> x2, local copies, waits for them, and re-layouts: 6.01 us -> 7.15 us  [sent(): return blocks[picked.reshape(-1)].reshape(n, -1, width)]
  transfers between devices with their start and end apart: 1 -> 2, of which waited for: 0 -> 2; matrix products, arithmetic and copies ran while one was open for 9% -> 8% of each run, Pallas kernels for 59% -> 0%
where the time goes in v2:
time: 272 us; the launch traced here: 271 us
  Pallas kernels  105 us (39%)
  waiting for transfers between devices  98 us (36%)
  matrix products  32.3 us (12%)
  local copies, waits for them, and re-layouts  23.4 us (9%)
  starting transfers between devices  8.47 us (3%)
  other arithmetic  3.81 us (1%)
    all_to_all x2, waiting for transfers between devices, exchange(): lax.all_to_all(outgoing, 'ctx', split_axis=0, concat_axis=0, tiled=True)  98 us
    pallas_call x1, Pallas kernels, per_device(): pl.pallas_call(functools.partial(rim_kernel, n, rows), out_shape=(jax.Sha...  57.1 us
    pallas_call x1, Pallas kernels, per_device(): pl.pallas_call(functools.partial(attend_kernel, n_local, width), out_shap...  22.6 us
    dot_general x2, matrix products, project(): jnp.dot(rows_in.reshape(-1, width), kv_weight, preferred_element_type=jnp...  19.9 us
    pallas_call x1, Pallas kernels, per_device(): pl.pallas_call(functools.partial(collect_kernel, n), out_shape=(jax.Shape...  19.1 us
    dot_general x1, matrix products, per_device(): jnp.dot(rimmed, qkv_weight, preferred_element_type=jnp.float32)  9.41 us
    all_to_all x2, starting transfers between devices, exchange(): lax.all_to_all(outgoing, 'ctx', split_axis=0, concat_axis=0, tiled=True)  8.47 us
    gather x2, local copies, waits for them, and re-layouts, sent(): return blocks[picked.reshape(-1)].reshape(n, -1, width)  7.15 us
  transfers between devices with their start and end apart: 2, of which 2 were waited for; matrix products, arithmetic and copies ran while one was open for 8% of the time, Pallas kernels for 0%

profile of v2, /device:TPU:0, one launch (start us, length us, event | category | flops | bytes accessed | tf_op | source)
XLA Modules:
  0.0 271.4 jit_solution(4140651644493637645)
XLA Ops:
  0.0 0.0 copy-start
  0.0 0.9 copy.19
  0.9 0.7 broadcast_multiply_fusion
  1.6 0.8 copy.22
  2.4 0.1 copy.21
  2.5 0.1 mul.47
  2.6 0.1 reshape.125
  2.7 0.1 reshape.156
  2.7 0.1 fusion.7
  2.8 0.1 reduce_window_sum.11
  2.9 0.2 select_reduce_fusion
  3.1 0.7 scatter_custom_fusion
  3.8 0.1 reshape.127
  3.9 0.6 pad.4.t_ref
  4.5 57.1 %rim.1 = (bf16[1024,1024]{1,0:T(8,128)(2,1)}, s32[8,8,128]{2,1,0:T(8,128)}) custom-call(bf16[768,1024]{1,0:T(8,128)(2,1)} %x_ref.1, s32[8,8,128]{2,1,0:T(8,128)} %pad.4.t_ref), custom_call_target="tpu_custom_call" | custom-call | tf_op jit(solution)/shard_map/rim/pallas_call | solution.py:262
  61.6 0.8 slice.18
  62.4 0.2 fusion.8
  62.6 9.4 %convolution_convert_fusion.1.p_ref = bf16[1024,3072]{1,0:T(8,128)(2,1)S(1)} fusion(bf16[1024,1024]{1,0:T(8,128)(2,1)} %get-tuple-element.13, bf16[1024,3072]{1,0:T(8,128)(2,1)} %param.7), kind=kOutput, calls=%fused_computation.4 | convolution fusion | flops 6445596672 | bytes 14680064 | tf_op jit(solution)/shard_map/dot_general | solution.py:286
  72.0 6.4 %partial.1 = (bf16[2,64,1024]{2,1,0:T(8,128)(2,1)S(1)}, f32[8,256]{1,0:T(8,128)S(1)}) custom-call(bf16[1024,3072]{1,0:T(8,128)(2,1)S(1)} %convolution_convert_fusion.1.p_ref), custom_call_target="tpu_custom_call" | custom-call | flops 1000000000 | bytes 7000000 | tf_op jit(solution)/shard_map/partial/pallas_call | solution.py:288
  78.4 0.0 copy-start.1
  78.4 2.7 copy-done.1
  81.1 0.7 copy-done.3
  81.8 0.6 copy-done.4
  82.4 3.0 %gather_fusion.1 = bf16[8,64,1024]{2,1,0:T(8,128)(2,1)} fusion(bf16[12,64,1024]{2,1,0:T(8,128)(2,1)} %bitcast.29, s32[1024]{0:T(1024)S(1)} %pad_clamp_fusion), kind=kCustom, calls=%fused_computation.1 | custom fusion | bytes 2097184 | tf_op jit(solution)/shard_map/gather | solution.py:279
  85.4 19.1 %collect.1 = (bf16[8,64,1024]{2,1,0:T(8,128)(2,1)}, f32[8,8,256]{2,1,0:T(8,128)}) custom-call(bf16[2,64,1024]{2,1,0:T(8,128)(2,1)} %copy-done.3, f32[8,256]{1,0:T(8,128)} %copy-done.4), custom_call_target="tpu_custom_call" | custom-call | tf_op jit(solution)/shard_map/collect/pallas_call | solution.py:298
  104.5 3.6 %all-to-all-start.1 = ((bf16[8,64,1024]{2,1,0:T(8,128)(2,1)}), bf16[8,64,1024]{2,1,0:T(8,128)(2,1)S(1)}, u32[]{:S(2)}, u32[]{:S(2)}) async-start(bf16[8,64,1024]{2,1,0:T(8,128)(2,1)} %gather_fusion.1), calls=%async_computation.1 | async-start | bytes 2097152 | tf_op jit(solution)/shard_map/all_to_all | solution.py:282
  108.1 0.1 reshape.129
  108.2 4.2 %gather_fusion = bf16[32,64,1024]{2,1,0:T(8,128)(2,1)} fusion(bf16[12,64,1024]{2,1,0:T(8,128)(2,1)} %bitcast.30, s32[1024]{0:T(1024)S(1)} %pad_clamp_fusion.1), kind=kCustom, calls=%fused_computation | custom fusion | bytes 8388736 | tf_op jit(solution)/shard_map/gather | solution.py:279
  112.4 21.9 %all-to-all-done.1 = bf16[8,64,1024]{2,1,0:T(8,128)(2,1)S(1)} async-done(((bf16[8,64,1024]{2,1,0:T(8,128)(2,1)}), bf16[8,64,1024]{2,1,0:T(8,128)(2,1)S(1)}, u32[]{:S(2)}, u32[]{:S(2)}) %all-to-all-start.1) | async-done | bytes 1048608 | tf_op jit(solution)/shard_map/all_to_all | solution.py:282
  134.3 4.9 %all-to-all-start = ((bf16[8,256,1024]{2,1,0:T(8,128)(2,1)}), bf16[8,256,1024]{2,1,0:T(8,128)(2,1)}, u32[]{:S(2)}, u32[]{:S(2)}) async-start(bf16[8,256,1024]{2,1,0:T(8,128)(2,1)} %bitcast.31), calls=%async_computation | async-start | bytes 8388608 | tf_op jit(solution)/shard_map/all_to_all | solution.py:282
  139.2 0.1 pad.8.clone
  139.3 0.1 add_add_fusion
  139.5 0.1 copy.20
  139.5 0.1 reshape.135.usable
  139.6 0.0 copy-done.5
  139.7 0.1 reshape.133
  139.8 0.1 fusion.13
  140.0 0.1 copy.24
  140.1 2.6 broadcast_in_dim.33
  142.7 4.9 %reshape.134 = f32[8,64,1024]{2,1,0:T(8,128)} reshape(f32[8,64,16,64]{3,2,1,0:T(8,128)} %broadcast_in_dim.33) | data formatting | bytes 4194304 | tf_op jit(solution)/shard_map/reshape | solution.py:318
  147.6 2.2 multiply_reduce_fusion.glob_ref
  149.8 5.8 %fusion.3.b0.b1.b2 = bf16[512,2048]{1,0:T(8,128)(2,1)} fusion(bf16[512,1024]{1,0:T(8,128)(2,1)S(1)} %bitcast.32, bf16[1024,3072]{1,0:T(8,128)(2,1)} %param.7), kind=kOutput, calls=%fused_computation.8 | convolution fusion | flops 2148532224 | bytes 7340032 | tf_op jit(solution)/shard_map/dot_general | solution.py:336
  155.7 76.1 %all-to-all-done = bf16[8,256,1024]{2,1,0:T(8,128)(2,1)} async-done(((bf16[8,256,1024]{2,1,0:T(8,128)(2,1)}), bf16[8,256,1024]{2,1,0:T(8,128)(2,1)}, u32[]{:S(2)}, u32[]{:S(2)}) %all-to-all-start) | async-done | bytes 4194336 | tf_op jit(solution)/shard_map/all_to_all | solution.py:282
  231.8 14.1 %convolution_convert_fusion.a0.a1.a2 = bf16[2048,2048]{1,0:T(8,128)(2,1)} fusion(bf16[2048,1024]{1,0:T(8,128)(2,1)} %bitcast.7, bf16[1024,3072]{1,0:T(8,128)(2,1)} %param.7), kind=kOutput, calls=%fused_computation.3 | convolution fusion | flops 8594128896 | bytes 16777216 | tf_op jit(solution)/shard_map/dot_general | solution.py:336
  245.9 0.0 slice-done
  245.9 0.0 slice-done.1
  245.9 22.6 %attend.1 = bf16[768,1024]{1,0:T(8,128)(2,1)S(1)} custom-call(s32[36]{0:T(128)S(1)} %compare_select_fusion.4.sa, s32[36]{0:T(128)S(1)} %get-tuple-element.25.sb, s32[36]{0:T(128)S(1)} %get-tuple-element.23.late, s32[96]{0:T(128)S(1)} %reshape.135.usable, s32[12]{0:T(128)S(1)} %or_convert_fusion.use_glob, bf16[1024,3072]{1,0:T(8,128)(2,1)S(1)} %bitcast.28, ...), custom_call_target="tpu_custom_call" | custom-call | tf_op jit(solution)/shard_map/attend/pallas_call | solution.py:351
  268.5 2.9 %convolution_convert_fusion.2 = bf16[768,1024]{1,0:T(8,128)(2,1)} fusion(bf16[768,1024]{1,0:T(8,128)(2,1)S(1)} %attend.1, bf16[1024,1024]{1,0:T(8,128)(2,1)S(1)} %copy-done), kind=kOutput, calls=%fused_computation.10 | convolution fusion | flops 1611399168 | bytes 5242880 | tf_op jit(solution)/shard_map/dot_general | solution.py:386
  (29 shorter events, 0.2 us)
Async XLA Ops:
  0.0 268.5 %copy-start = (bf16[1024,1024]{1,0:T(8,128)(2,1)S(1)}, bf16[1024,1024]{1,0:T(8,128)(2,1)}, u32[]{:S(2)}) copy-start(bf16[1024,1024]{1,0:T(8,128)(2,1)} %param.8) | copy-start | bytes 6291460
  78.4 2.7 copy-start.1
  81.1 0.7 copy-start.3
  81.8 0.6 copy-start.4
  104.5 29.7 %all-to-all-start.1 = ((bf16[8,64,1024]{2,1,0:T(8,128)(2,1)}), bf16[8,64,1024]{2,1,0:T(8,128)(2,1)S(1)}, u32[]{:S(2)}, u32[]{:S(2)}) async-start(bf16[8,64,1024]{2,1,0:T(8,128)(2,1)} %gather_fusion.1), calls=%async_computation.1 | async-start | bytes 2097152 | tf_op jit(solution)/shard_map/all_to_all | solution.py:282
  134.3 5.4 %copy-start.5 = (f32[8,8,256]{2,1,0:T(8,128)S(1)}, f32[8,8,256]{2,1,0:T(8,128)}, u32[]{:S(2)}) copy-start(f32[8,8,256]{2,1,0:T(8,128)} %get-tuple-element.20) | copy-start | bytes 196612
  134.3 97.5 %all-to-all-start = ((bf16[8,256,1024]{2,1,0:T(8,128)(2,1)}), bf16[8,256,1024]{2,1,0:T(8,128)(2,1)}, u32[]{:S(2)}, u32[]{:S(2)}) async-start(bf16[8,256,1024]{2,1,0:T(8,128)(2,1)} %bitcast.31), calls=%async_computation | async-start | bytes 8388608 | tf_op jit(solution)/shard_map/all_to_all | solution.py:282
  231.8 14.1 %slice-start = ((s8[6291456]{0:T(1024)(128)(4,1)}), s8[4194304]{0:T(1024)(128)(4,1)S(1)}, s32[]{:S(2)}) async-start(s8[6291456]{0:T(1024)(128)(4,1)} %bitcast.27), calls=%async_computation.2 | async-start | bytes 8388608
  231.8 14.1 %slice-start.1 = ((s8[6291456]{0:T(1024)(128)(4,1)}), s8[2097152]{0:T(1024)(128)(4,1)S(1)}, s32[]{:S(2)}) async-start(s8[6291456]{0:T(1024)(128)(4,1)} %bitcast.27), calls=%async_computation.3 | async-start | bytes 4194304
  231.8 14.1 %copy-start.2 = (bf16[512,2048]{1,0:T(8,128)(2,1)S(1)}, bf16[512,2048]{1,0:T(8,128)(2,1)}, u32[]{:S(2)}) copy-start(bf16[512,2048]{1,0:T(8,128)(2,1)} %fusion.3.b0.b1.b2) | copy-start | bytes 6291460

commit v3 on v1

--- a/solution.py
+++ b/solution.py
@@ -41,17 +41,21 @@
     )
 
 
-def rim_kernel(n, rows, x_ref, o_ref, own_sem, edge_sem, send_sem, halo_send, recv_sem):
+def rim_kernel(
+    n, rows, x_ref, t_ref, o_ref, a_ref, edge_sem, send_sem, halo_send, recv_sem, asks, asked
+):
     me = lax.axis_index("ctx")
     first = x_ref.at[pl.ds(0, BLOCK)]
     last = x_ref.at[pl.ds(rows - BLOCK, BLOCK)]
-    prev = o_ref.at[pl.ds(0, BLOCK)]
-    after = o_ref.at[pl.ds(rows + BLOCK, BLOCK)]
-    glob0 = o_ref.at[pl.ds(rows + 2 * BLOCK, BLOCK)]
-    glob1 = o_ref.at[pl.ds(rows + 3 * BLOCK, BLOCK)]
-    own = pltpu.make_async_copy(x_ref, o_ref.at[pl.ds(BLOCK, rows)], own_sem)
-    own.start()
+    prev, after, glob0, glob1 = (o_ref.at[pl.ds(b * BLOCK, BLOCK)] for b in range(4))
+    keep = pltpu.make_async_copy(t_ref.at[me], a_ref.at[me], asks.at[0])
+    keep.start()
     greet_all(me, n)
+    requests = []
+    for d in range(1, n):
+        to = lax.rem(me + d, n)
+        requests.append(remote(t_ref.at[to], a_ref.at[me], asks.at[d], asked.at[d], to))
+        requests[-1].start()
     up, down = lax.rem(me + 1, n), lax.rem(me + n - 1, n)
     to_next = remote(last, prev, halo_send.at[0], recv_sem.at[0], up)
     to_prev = remote(first, after, halo_send.at[1], recv_sem.at[1], down)
@@ -108,7 +112,11 @@
         to_prev.wait_recv()
         remote(last, glob1, send_sem.at[0], recv_sem.at[3], up).wait_recv()
 
-    own.wait()
+    for d in range(1, n):
+        requests[d - 1].wait_send()
+        source = lax.rem(me + n - d, n)
+        remote(t_ref.at[source], a_ref.at[source], asks.at[d], asked.at[d], source).wait_recv()
+    keep.wait()
 
 
 def partial_kernel(rows, width, p_ref, o_ref, lse_ref):
@@ -239,22 +247,26 @@
 
     slot_ids = request_slots(rand_owner, n, capacity)
     table = jnp.zeros((n * capacity,), jnp.int32).at[slot_ids].set(rand_local.reshape(-1))
-    asked_for = lax.all_to_all(
-        table.reshape(n, capacity), "ctx", split_axis=0, concat_axis=0, tiled=True
-    )
+    table = jnp.pad(table.reshape(n, 1, capacity), ((0, 0), (0, 7), (0, 128 - capacity)))
+
+    edges, asked_for = pl.pallas_call(
+        functools.partial(rim_kernel, n, rows),
+        out_shape=(
+            jax.ShapeDtypeStruct((4 * BLOCK, width), inputs.dtype),
+            jax.ShapeDtypeStruct(table.shape, table.dtype),
+        ),
+        in_specs=[any_spec] * 2,
+        out_specs=(any_spec, any_spec),
+        scratch_shapes=[dma((2,)), dma((n,)), dma((2,)), dma((4,)), dma((n,)), dma((n,))],
+        compiler_params=pltpu.CompilerParams(collective_id=0, has_side_effects=True),
+        name="rim",
+    )(inputs, table)
+    asked_for = asked_for[:, 0, :capacity]
     outgoing = inputs.reshape(n_local, BLOCK, width)[asked_for.reshape(-1)]
     outgoing = outgoing.reshape(n, capacity * BLOCK, width)
+    outgoing, edges = lax.optimization_barrier((outgoing, edges))
     arrived = lax.all_to_all(outgoing, "ctx", split_axis=0, concat_axis=0, tiled=True)
-
-    rimmed = pl.pallas_call(
-        functools.partial(rim_kernel, n, rows),
-        out_shape=jax.ShapeDtypeStruct((rows + 4 * BLOCK, width), inputs.dtype),
-        in_specs=[any_spec],
-        out_specs=any_spec,
-        scratch_shapes=[dma, dma((2,)), dma((n,)), dma((2,)), dma((4,))],
-        compiler_params=pltpu.CompilerParams(collective_id=0, has_side_effects=True),
-        name="rim",
-    )(inputs)
+    rimmed = jnp.concatenate([edges[:BLOCK], inputs, edges[BLOCK:]], axis=0)
     near = jnp.dot(rimmed, qkv_weight, preferred_element_type=jnp.float32).astype(jnp.bfloat16)
 
     part, lse = pl.pallas_call(

time: 241 us -> 221 us (0.917)
  blocking collectives: 13.5 us -> 0 us
  Pallas kernels: 164 us -> 155 us
    pallas_call x1, Pallas kernels: 101 us -> 23.9 us  [per_device(): pl.pallas_call(functools.partial(rim_kernel, n, rows), out_shape=(jax.Sha...]
    pallas_call x1, Pallas kernels: 33.7 us -> 102 us  [per_device(): pl.pallas_call(functools.partial(collect_kernel, n), out_shape=(jax.Shape...]
    all_to_all x1 -> x0, blocking collectives: 13.5 us -> none  [per_device(): lax.all_to_all(table.reshape(n, capacity), 'ctx', split_axis=0, concat_ax...]
    unnamed x14 -> x16, local copies, waits for them, and re-layouts: 8.34 us -> 8.35 us
  transfers between devices with their start and end apart: 1 -> 1, of which waited for: 0 -> 0; matrix products, arithmetic and copies ran while one was open for 9% -> 9% of each run, Pallas kernels for 59% -> 49%
where the time goes in v3:
time: 221 us
  Pallas kernels  155 us (70%)
  matrix products  29.2 us (13%)
  local copies, waits for them, and re-layouts  25.1 us (11%)
  starting transfers between devices  6.62 us (3%)
  other arithmetic  4.2 us (2%)
    pallas_call x1, Pallas kernels, per_device(): pl.pallas_call(functools.partial(collect_kernel, n), out_shape=(jax.Shape...  102 us
    pallas_call x1, Pallas kernels, per_device(): pl.pallas_call(functools.partial(rim_kernel, n, rows), out_shape=(jax.Sha...  23.9 us
    pallas_call x1, Pallas kernels, per_device(): pl.pallas_call(functools.partial(attend_kernel, n_local, width), out_shap...  22.5 us
    dot_general x1, matrix products, per_device(): jnp.dot(arrived.reshape(n * capacity * BLOCK, width), qkv_weight[:, width...  17 us
    dot_general x1, matrix products, per_device(): jnp.dot(rimmed, qkv_weight, preferred_element_type=jnp.float32)  9.24 us
    unnamed x16, local copies, waits for them, and re-layouts  8.35 us
    all_to_all x1, starting transfers between devices, per_device(): lax.all_to_all(outgoing, 'ctx', split_axis=0, concat_axis=0, tiled=True)  6.62 us
    pallas_call x1, Pallas kernels, per_device(): pl.pallas_call(functools.partial(partial_kernel, rows, width), out_shape=...  6.39 us
  transfers between devices with their start and end apart: 1, of which 0 were waited for; matrix products, arithmetic and copies ran while one was open for 9% of the time, Pallas kernels for 49%

profile of v3, /device:TPU:0, one launch (start us, length us, event | category | flops | bytes accessed | tf_op | source)
XLA Modules:
  0.0 220.5 jit_solution(4579327119938972688)
XLA Ops:
  0.0 0.0 copy-start
  0.0 0.9 copy.19
  0.9 0.7 broadcast_multiply_fusion
  1.6 0.8 copy.22
  2.4 0.1 reshape.118
  2.5 0.1 fusion.7
  2.6 0.1 reduce_window_sum.11
  2.6 0.2 select_reduce_fusion
  2.8 0.1 copy.21
  2.9 0.1 mul.43
  3.0 0.1 reshape.139
  3.1 0.7 scatter_custom_fusion
  3.8 0.1 reshape.121
  3.9 0.6 pad.4.t_ref
  4.5 23.9 %rim.1 = (bf16[256,1024]{1,0:T(8,128)(2,1)}, s32[8,8,128]{2,1,0:T(8,128)}) custom-call(bf16[768,1024]{1,0:T(8,128)(2,1)} %x_ref.1, s32[8,8,128]{2,1,0:T(8,128)} %pad.4.t_ref), custom_call_target="tpu_custom_call" | custom-call | tf_op jit(solution)/shard_map/rim/pallas_call | solution.py:252
  28.4 0.8 slice_reduce_fusion
  29.2 0.1 reshape_squeeze.3
  29.3 6.0 %gather_fusion = bf16[40,64,1024]{2,1,0:T(8,128)(2,1)} fusion(bf16[12,64,1024]{2,1,0:T(8,128)(2,1)} %bitcast.21, s32[1024]{0:T(1024)S(1)} %pad_clamp_fusion), kind=kCustom, calls=%fused_computation | custom fusion | bytes 10485920 | tf_op jit(solution)/shard_map/gather | solution.py:265
  35.3 0.0 copy-start.6
  35.3 6.6 %all-to-all-start = ((bf16[8,320,1024]{2,1,0:T(8,128)(2,1)}), bf16[8,320,1024]{2,1,0:T(8,128)(2,1)}, u32[]{:S(2)}, u32[]{:S(2)}) async-start(bf16[8,320,1024]{2,1,0:T(8,128)(2,1)} %bitcast.22), calls=%async_computation | async-start | bytes 10485760 | tf_op jit(solution)/shard_map/all_to_all | solution.py:268
  41.9 0.0 copy-done.6
  42.0 9.2 %convolution_convert_fusion.1.p_ref = bf16[1024,3072]{1,0:T(8,128)(2,1)S(1)} fusion(bf16[1024,3072]{1,0:T(8,128)(2,1)} %param.7, bf16[192,1024]{1,0:T(8,128)(2,1)S(1)} %slice.20, bf16[768,1024]{1,0:T(8,128)(2,1)} %x_ref.1, bf16[64,1024]{1,0:T(8,128)(2,1)S(1)} %slice.19), kind=kOutput, calls=%fused_computation.3 | convolution fusion | flops 6451888128 | bytes 14680064 | tf_op jit(solution)/shard_map/dot_general | solution.py:270
  51.2 6.4 %partial.1 = (bf16[2,64,1024]{2,1,0:T(8,128)(2,1)S(1)}, f32[8,256]{1,0:T(8,128)S(1)}) custom-call(bf16[1024,3072]{1,0:T(8,128)(2,1)S(1)} %convolution_convert_fusion.1.p_ref), custom_call_target="tpu_custom_call" | custom-call | flops 1000000000 | bytes 7000000 | tf_op jit(solution)/shard_map/partial/pallas_call | solution.py:272
  57.6 0.0 copy-start.1
  57.6 2.6 %copy-done.1 = bf16[1024,3072]{1,0:T(8,128)(2,1)} copy-done((bf16[1024,3072]{1,0:T(8,128)(2,1)}, bf16[1024,3072]{1,0:T(8,128)(2,1)S(1)}, u32[]{:S(2)}) %copy-start.1) | copy-done | bytes 6291480
  60.2 0.0 copy-start.3
  60.2 0.7 copy-done.3
  60.9 0.0 copy-start.4
  60.9 0.6 copy-done.4
  61.5 102.4 %collect.1 = (bf16[8,64,1024]{2,1,0:T(8,128)(2,1)}, f32[8,8,256]{2,1,0:T(8,128)}) custom-call(bf16[2,64,1024]{2,1,0:T(8,128)(2,1)} %copy-done.3, f32[8,256]{1,0:T(8,128)} %copy-done.4), custom_call_target="tpu_custom_call" | custom-call | tf_op jit(solution)/shard_map/collect/pallas_call | solution.py:282
  163.9 0.9 broadcast_select_fusion.1
  164.7 0.1 reshape.124
  164.9 0.1 fusion.13
  165.1 0.1 copy.24
  165.2 2.6 %broadcast_in_dim.24 = f32[8,64,16,64]{3,2,1,0:T(8,128)} broadcast(f32[8,64,16]{2,1,0:T(8,128)S(1)} %copy.24), dimensions={0,1,2} | broadcast | bytes 2129920 | tf_op jit(solution)/shard_map/broadcast_in_dim | solution.py:300
  167.8 5.0 %reshape.125 = f32[8,64,1024]{2,1,0:T(8,128)} reshape(f32[8,64,16,64]{3,2,1,0:T(8,128)} %broadcast_in_dim.24) | data formatting | bytes 4194304 | tf_op jit(solution)/shard_map/reshape | solution.py:300
  172.8 0.1 pad.11.clone
  172.9 0.1 add_add_fusion
  173.0 0.1 copy.20
  173.1 0.1 reshape.126.usable
  173.2 0.0 copy-done.5
  173.2 2.0 multiply_reduce_fusion.glob_ref
  175.2 0.0 all-to-all-done
  175.2 17.0 %convolution_convert_fusion.r0.r1.r2 = bf16[2560,2048]{1,0:T(8,128)(2,1)} fusion(bf16[2560,1024]{1,0:T(8,128)(2,1)} %bitcast.6, bf16[1024,3072]{1,0:T(8,128)(2,1)} %param.7), kind=kOutput, calls=%fused_computation.2 | convolution fusion | flops 10742661120 | bytes 19922944 | tf_op jit(solution)/shard_map/dot_general | solution.py:315
  192.3 2.8 %copy-done.2 = bf16[1024,3072]{1,0:T(8,128)(2,1)S(1)} copy-done((bf16[1024,3072]{1,0:T(8,128)(2,1)S(1)}, bf16[1024,3072]{1,0:T(8,128)(2,1)}, u32[]{:S(2)}) %copy-start.2) | copy-done | bytes 6291480
  195.1 22.5 %attend.1 = bf16[768,1024]{1,0:T(8,128)(2,1)S(1)} custom-call(s32[36]{0:T(128)S(1)} %multiply_add_fusion.1.slots, s32[96]{0:T(128)S(1)} %reshape.126.usable, s32[12]{0:T(128)S(1)} %or_convert_fusion.use_glob, bf16[1024,3072]{1,0:T(8,128)(2,1)S(1)} %copy-done.2, bf16[2560,2048]{1,0:T(8,128)(2,1)} %convolution_convert_fusion.r0.r1.r2, ...), custom_call_target="tpu_custom_call" | custom-call | tf_op jit(solution)/shard_map/attend/pallas_call | solution.py:324
  217.6 0.0 copy-done
  217.6 2.9 %convolution_convert_fusion.2 = bf16[768,1024]{1,0:T(8,128)(2,1)} fusion(bf16[768,1024]{1,0:T(8,128)(2,1)S(1)} %attend.1, bf16[1024,1024]{1,0:T(8,128)(2,1)S(1)} %copy-done), kind=kOutput, calls=%fused_computation.11 | convolution fusion | flops 1611399168 | bytes 5242880 | tf_op jit(solution)/shard_map/dot_general | solution.py:351
  (20 shorter events, 0.2 us)
Async XLA Ops:
  0.0 217.6 %copy-start = (bf16[1024,1024]{1,0:T(8,128)(2,1)S(1)}, bf16[1024,1024]{1,0:T(8,128)(2,1)}, u32[]{:S(2)}) copy-start(bf16[1024,1024]{1,0:T(8,128)(2,1)} %param.8) | copy-start | bytes 6291460
  35.3 6.6 %copy-start.6 = (bf16[256,1024]{1,0:T(8,128)(2,1)S(1)}, bf16[256,1024]{1,0:T(8,128)(2,1)}, u32[]{:S(2)}) copy-start(bf16[256,1024]{1,0:T(8,128)(2,1)} %get-tuple-element.15) | copy-start | bytes 1572868
  35.3 139.9 %all-to-all-start = ((bf16[8,320,1024]{2,1,0:T(8,128)(2,1)}), bf16[8,320,1024]{2,1,0:T(8,128)(2,1)}, u32[]{:S(2)}, u32[]{:S(2)}) async-start(bf16[8,320,1024]{2,1,0:T(8,128)(2,1)} %bitcast.22), calls=%async_computation | async-start | bytes 10485760 | tf_op jit(solution)/shard_map/all_to_all | solution.py:268
  57.6 2.6 %copy-start.1 = (bf16[1024,3072]{1,0:T(8,128)(2,1)}, bf16[1024,3072]{1,0:T(8,128)(2,1)S(1)}, u32[]{:S(2)}) copy-start(bf16[1024,3072]{1,0:T(8,128)(2,1)S(1)} %convolution_convert_fusion.1.p_ref) | copy-start | bytes 18874372
  60.2 0.7 copy-start.3
  60.9 0.6 copy-start.4
  167.8 5.4 %copy-start.5 = (bf16[8,64,1024]{2,1,0:T(8,128)(2,1)S(1)}, bf16[8,64,1024]{2,1,0:T(8,128)(2,1)}, u32[]{:S(2)}) copy-start(bf16[8,64,1024]{2,1,0:T(8,128)(2,1)} %get-tuple-element.19) | copy-start | bytes 3145732
  192.3 2.8 %copy-start.2 = (bf16[1024,3072]{1,0:T(8,128)(2,1)S(1)}, bf16[1024,3072]{1,0:T(8,128)(2,1)}, u32[]{:S(2)}) copy-start(bf16[1024,3072]{1,0:T(8,128)(2,1)} %copy-done.1) | copy-start | bytes 18874372

commit v4 on v2

--- a/solution.py
+++ b/solution.py
@@ -42,17 +42,12 @@
 
 
 def rim_kernel(
-    n, rows, x_ref, t_ref, o_ref, a_ref, own_sem, edge_sem, send_sem, halo_send, recv_sem, asks, asked
+    n, rows, x_ref, t_ref, o_ref, a_ref, edge_sem, send_sem, halo_send, recv_sem, asks, asked
 ):
     me = lax.axis_index("ctx")
     first = x_ref.at[pl.ds(0, BLOCK)]
     last = x_ref.at[pl.ds(rows - BLOCK, BLOCK)]
-    prev = o_ref.at[pl.ds(0, BLOCK)]
-    after = o_ref.at[pl.ds(rows + BLOCK, BLOCK)]
-    glob0 = o_ref.at[pl.ds(rows + 2 * BLOCK, BLOCK)]
-    glob1 = o_ref.at[pl.ds(rows + 3 * BLOCK, BLOCK)]
-    own = pltpu.make_async_copy(x_ref, o_ref.at[pl.ds(BLOCK, rows)], own_sem)
-    own.start()
+    prev, after, glob0, glob1 = (o_ref.at[pl.ds(b * BLOCK, BLOCK)] for b in range(4))
     keep = pltpu.make_async_copy(t_ref.at[me], a_ref.at[me], asks.at[0])
     keep.start()
     greet_all(me, n)
@@ -122,7 +117,6 @@
         source = lax.rem(me + n - d, n)
         remote(t_ref.at[source], a_ref.at[source], asks.at[d], asked.at[d], source).wait_recv()
     keep.wait()
-    own.wait()
 
 
 def partial_kernel(rows, width, p_ref, o_ref, lse_ref):
@@ -259,15 +253,15 @@
     table = jnp.zeros((n * capacity,), jnp.int32).at[slot_ids].set(rand_local.reshape(-1))
     table = jnp.pad(table.reshape(n, 1, capacity), ((0, 0), (0, 7), (0, 128 - capacity)))
 
-    rimmed, asked_for = pl.pallas_call(
+    edges, asked_for = pl.pallas_call(
         functools.partial(rim_kernel, n, rows),
         out_shape=(
-            jax.ShapeDtypeStruct((rows + 4 * BLOCK, width), inputs.dtype),
+            jax.ShapeDtypeStruct((4 * BLOCK, width), inputs.dtype),
             jax.ShapeDtypeStruct(table.shape, table.dtype),
         ),
         in_specs=[any_spec] * 2,
         out_specs=(any_spec, any_spec),
-        scratch_shapes=[dma, dma((2,)), dma((n,)), dma((2,)), dma((4,)), dma((n,)), dma((n,))],
+        scratch_shapes=[dma((2,)), dma((n,)), dma((2,)), dma((4,)), dma((n,)), dma((n,))],
         compiler_params=pltpu.CompilerParams(collective_id=0, has_side_effects=True),
         name="rim",
     )(inputs, table)
@@ -281,8 +275,11 @@
     def exchange(outgoing):
         return lax.all_to_all(outgoing, "ctx", split_axis=0, concat_axis=0, tiled=True)
 
-    outgoing_b = sent(asked_for[:, head:])
-    arrived_a = exchange(sent(asked_for[:, :head]))
+    outgoing_a, outgoing_b, edges = lax.optimization_barrier(
+        (sent(asked_for[:, :head]), sent(asked_for[:, head:]), edges)
+    )
+    arrived_a = exchange(outgoing_a)
+    rimmed = jnp.concatenate([edges[:BLOCK], inputs, edges[BLOCK:]], axis=0)
     near = jnp.dot(rimmed, qkv_weight, preferred_element_type=jnp.float32).astype(jnp.bfloat16)
 
     part, lse = pl.pallas_call(
@@ -307,7 +304,7 @@
         compiler_params=pltpu.CompilerParams(collective_id=1, has_side_effects=True),
         name="collect",
     )(part, lse)
-    outgoing_b, parts = lax.optimization_barrier((outgoing_b, parts))
+    outgoing_b, arrived_a, parts = lax.optimization_barrier((outgoing_b, arrived_a, parts))
     arrived_b = exchange(outgoing_b)
     is_first, is_last = me == 0, me == n - 1
     gather_here = is_first | is_last

time: 272 us -> 213 us (0.78)
  waiting for transfers between devices: 98 us -> 9.32 us
  Pallas kernels: 105 us -> 133 us
    all_to_all x2, waiting for transfers between devices: 98 us -> 9.32 us  [exchange(): lax.all_to_all(outgoing, 'ctx', split_axis=0, concat_axis=0, tiled=True)]
    pallas_call x1, Pallas kernels: 19.1 us -> 79.8 us  [per_device(): pl.pallas_call(functools.partial(collect_kernel, n), out_shape=(jax.Shape...]
    pallas_call x1, Pallas kernels: 57.1 us -> 23.9 us  [per_device(): pl.pallas_call(functools.partial(rim_kernel, n, rows), out_shape=(jax.Sha...]
  transfers between devices with their start and end apart: 2 -> 2, of which waited for: 2 -> 1; matrix products, arithmetic and copies ran while one was open for 8% -> 16% of each run, Pallas kernels for 0% -> 41%
where the time goes in v4:
time: 213 us
  Pallas kernels  133 us (62%)
  matrix products  31.1 us (15%)
  local copies, waits for them, and re-layouts  23.7 us (11%)
  starting transfers between devices  11 us (5%)
  waiting for transfers between devices  9.32 us (4%)
  other arithmetic  4.41 us (2%)
    pallas_call x1, Pallas kernels, per_device(): pl.pallas_call(functools.partial(collect_kernel, n), out_shape=(jax.Shape...  79.8 us
    pallas_call x1, Pallas kernels, per_device(): pl.pallas_call(functools.partial(rim_kernel, n, rows), out_shape=(jax.Sha...  23.9 us
    pallas_call x1, Pallas kernels, per_device(): pl.pallas_call(functools.partial(attend_kernel, n_local, width), out_shap...  22.6 us
    dot_general x2, matrix products, project(): jnp.dot(rows_in.reshape(-1, width), kv_weight, preferred_element_type=jnp...  18.9 us
    all_to_all x2, starting transfers between devices, exchange(): lax.all_to_all(outgoing, 'ctx', split_axis=0, concat_axis=0, tiled=True)  11 us
    all_to_all x2, waiting for transfers between devices, exchange(): lax.all_to_all(outgoing, 'ctx', split_axis=0, concat_axis=0, tiled=True)  9.32 us
    dot_general x1, matrix products, per_device(): jnp.dot(rimmed, qkv_weight, preferred_element_type=jnp.float32)  9.23 us
    gather x2, local copies, waits for them, and re-layouts, sent(): return blocks[picked.reshape(-1)].reshape(n, -1, width)  7.29 us
  transfers between devices with their start and end apart: 2, of which 1 were waited for; matrix products, arithmetic and copies ran while one was open for 16% of the time, Pallas kernels for 41%

profile of v4, /device:TPU:0, one launch (start us, length us, event | category | flops | bytes accessed | tf_op | source)
XLA Modules:
  0.0 212.5 jit_solution(13182898932949968102)
XLA Ops:
  0.0 0.0 copy-start
  0.0 0.9 copy.19
  0.9 0.7 broadcast_multiply_fusion
  1.6 0.8 copy.22
  2.4 0.1 reshape.125
  2.5 0.1 fusion.12
  2.5 0.1 reduce_window_sum.11
  2.6 0.2 select_reduce_fusion
  2.8 0.1 copy.21
  2.9 0.1 mul.47
  3.0 0.1 reshape.156
  3.1 0.7 scatter_custom_fusion
  3.8 0.1 reshape.128
  3.9 0.6 pad.4.t_ref
  4.5 23.9 %rim.1 = (bf16[256,1024]{1,0:T(8,128)(2,1)}, s32[8,8,128]{2,1,0:T(8,128)}) custom-call(bf16[768,1024]{1,0:T(8,128)(2,1)} %x_ref.1, s32[8,8,128]{2,1,0:T(8,128)} %pad.4.t_ref), custom_call_target="tpu_custom_call" | custom-call | tf_op jit(solution)/shard_map/rim/pallas_call | solution.py:256
  28.4 0.8 slice.24
  29.2 0.2 fusion.13
  29.4 0.1 reshape.129
  29.5 4.3 %gather_fusion = bf16[32,64,1024]{2,1,0:T(8,128)(2,1)} fusion(bf16[12,64,1024]{2,1,0:T(8,128)(2,1)} %bitcast.27, s32[1024]{0:T(1024)S(1)} %pad_clamp_fusion.1), kind=kCustom, calls=%fused_computation | custom fusion | bytes 8388736 | tf_op jit(solution)/shard_map/gather | solution.py:273
  33.8 3.0 %gather_fusion.1 = bf16[8,64,1024]{2,1,0:T(8,128)(2,1)} fusion(bf16[12,64,1024]{2,1,0:T(8,128)(2,1)} %bitcast.28, s32[1024]{0:T(1024)S(1)} %pad_clamp_fusion), kind=kCustom, calls=%fused_computation.1 | custom fusion | bytes 2097184 | tf_op jit(solution)/shard_map/gather | solution.py:273
  36.8 6.6 %all-to-all-start = ((bf16[8,256,1024]{2,1,0:T(8,128)(2,1)}), bf16[8,256,1024]{2,1,0:T(8,128)(2,1)}, u32[]{:S(2)}, u32[]{:S(2)}) async-start(bf16[8,256,1024]{2,1,0:T(8,128)(2,1)} %bitcast.29), calls=%async_computation | async-start | bytes 8388608 | tf_op jit(solution)/shard_map/all_to_all | solution.py:276
  43.4 0.0 copy-done.5
  43.4 9.2 %convolution_convert_fusion.1.p_ref = bf16[1024,3072]{1,0:T(8,128)(2,1)S(1)} fusion(bf16[1024,3072]{1,0:T(8,128)(2,1)} %param.7, bf16[192,1024]{1,0:T(8,128)(2,1)S(1)} %slice.28, bf16[768,1024]{1,0:T(8,128)(2,1)} %x_ref.1, bf16[64,1024]{1,0:T(8,128)(2,1)S(1)} %slice.27), kind=kOutput, calls=%fused_computation.4 | convolution fusion | flops 6451888128 | bytes 14680064 | tf_op jit(solution)/shard_map/dot_general | solution.py:283
  52.7 6.4 %partial.1 = (bf16[2,64,1024]{2,1,0:T(8,128)(2,1)S(1)}, f32[8,256]{1,0:T(8,128)S(1)}) custom-call(bf16[1024,3072]{1,0:T(8,128)(2,1)S(1)} %convolution_convert_fusion.1.p_ref), custom_call_target="tpu_custom_call" | custom-call | flops 1000000000 | bytes 7000000 | tf_op jit(solution)/shard_map/partial/pallas_call | solution.py:285
  59.1 2.6 %copy-done.1 = bf16[1024,3072]{1,0:T(8,128)(2,1)} copy-done((bf16[1024,3072]{1,0:T(8,128)(2,1)}, bf16[1024,3072]{1,0:T(8,128)(2,1)S(1)}, u32[]{:S(2)}) %copy-start.1) | copy-done | bytes 6291480
  61.7 0.7 copy-done.2
  62.4 0.6 copy-done.3
  63.0 79.8 %collect.1 = (bf16[8,64,1024]{2,1,0:T(8,128)(2,1)}, f32[8,8,256]{2,1,0:T(8,128)}) custom-call(bf16[2,64,1024]{2,1,0:T(8,128)(2,1)} %copy-done.2, f32[8,256]{1,0:T(8,128)} %copy-done.3), custom_call_target="tpu_custom_call" | custom-call | tf_op jit(solution)/shard_map/collect/pallas_call | solution.py:295
  142.9 0.9 broadcast_select_fusion.1
  143.7 0.1 reshape.133
  143.8 0.1 fusion.19
  144.0 0.1 copy.24
  144.2 2.6 %broadcast_in_dim.33 = f32[8,64,16,64]{3,2,1,0:T(8,128)} broadcast(f32[8,64,16]{2,1,0:T(8,128)S(1)} %copy.24), dimensions={0,1,2} | broadcast | bytes 2129920 | tf_op jit(solution)/shard_map/broadcast_in_dim | solution.py:315
  146.8 5.0 %reshape.134 = f32[8,64,1024]{2,1,0:T(8,128)} reshape(f32[8,64,16,64]{3,2,1,0:T(8,128)} %broadcast_in_dim.33) | data formatting | bytes 4194304 | tf_op jit(solution)/shard_map/reshape | solution.py:315
  151.7 0.1 pad.11.clone
  151.9 0.1 add_add_fusion
  152.0 0.1 copy.20
  152.1 0.1 reshape.135.usable
  152.2 0.0 all-to-all-done
  152.3 4.4 %all-to-all-start.1 = ((bf16[8,64,1024]{2,1,0:T(8,128)(2,1)}), bf16[8,64,1024]{2,1,0:T(8,128)(2,1)}, u32[]{:S(2)}, u32[]{:S(2)}) async-start(bf16[8,64,1024]{2,1,0:T(8,128)(2,1)} %gather_fusion.1), calls=%async_computation.1 | async-start | bytes 2097152 | tf_op jit(solution)/shard_map/all_to_all | solution.py:276
  156.7 2.0 multiply_reduce_fusion.glob_ref
  158.7 13.9 %convolution_convert_fusion.a0.a1.a2 = bf16[2048,2048]{1,0:T(8,128)(2,1)} fusion(bf16[2048,1024]{1,0:T(8,128)(2,1)} %bitcast.7, bf16[1024,3072]{1,0:T(8,128)(2,1)} %param.7), kind=kOutput, calls=%fused_computation.3 | convolution fusion | flops 8594128896 | bytes 16777216 | tf_op jit(solution)/shard_map/dot_general | solution.py:333
  172.7 9.3 %all-to-all-done.1 = bf16[8,64,1024]{2,1,0:T(8,128)(2,1)} async-done(((bf16[8,64,1024]{2,1,0:T(8,128)(2,1)}), bf16[8,64,1024]{2,1,0:T(8,128)(2,1)}, u32[]{:S(2)}, u32[]{:S(2)}) %all-to-all-start.1) | async-done | bytes 1048608 | tf_op jit(solution)/shard_map/all_to_all | solution.py:276
  182.0 5.0 %fusion.3.b0.b1.b2 = bf16[512,2048]{1,0:T(8,128)(2,1)S(1)} fusion(bf16[512,1024]{1,0:T(8,128)(2,1)} %bitcast.8, bf16[1024,3072]{1,0:T(8,128)(2,1)} %param.7), kind=kOutput, calls=%fused_computation.8 | convolution fusion | flops 2148532224 | bytes 7340032 | tf_op jit(solution)/shard_map/dot_general | solution.py:333
  187.0 0.0 slice-done
  187.0 0.0 slice-done.1
  187.0 22.6 %attend.1 = bf16[768,1024]{1,0:T(8,128)(2,1)S(1)} custom-call(s32[36]{0:T(128)S(1)} %compare_select_fusion.4.sa, s32[36]{0:T(128)S(1)} %get-tuple-element.33.sb, s32[36]{0:T(128)S(1)} %get-tuple-element.31.late, s32[96]{0:T(128)S(1)} %reshape.135.usable, s32[12]{0:T(128)S(1)} %or_convert_fusion.use_glob, bf16[1024,3072]{1,0:T(8,128)(2,1)S(1)} %bitcast.26, ...), custom_call_target="tpu_custom_call" | custom-call | tf_op jit(solution)/shard_map/attend/pallas_call | solution.py:348
  209.6 2.9 %convolution_convert_fusion.2 = bf16[768,1024]{1,0:T(8,128)(2,1)} fusion(bf16[768,1024]{1,0:T(8,128)(2,1)S(1)} %attend.1, bf16[1024,1024]{1,0:T(8,128)(2,1)S(1)} %copy-done), kind=kOutput, calls=%fused_computation.15 | convolution fusion | flops 1611399168 | bytes 5242880 | tf_op jit(solution)/shard_map/dot_general | solution.py:383
  (31 shorter events, 0.3 us)
Async XLA Ops:
  0.0 209.6 %copy-start = (bf16[1024,1024]{1,0:T(8,128)(2,1)S(1)}, bf16[1024,1024]{1,0:T(8,128)(2,1)}, u32[]{:S(2)}) copy-start(bf16[1024,1024]{1,0:T(8,128)(2,1)} %param.8) | copy-start | bytes 6291460
  36.8 6.6 %copy-start.5 = (bf16[256,1024]{1,0:T(8,128)(2,1)S(1)}, bf16[256,1024]{1,0:T(8,128)(2,1)}, u32[]{:S(2)}) copy-start(bf16[256,1024]{1,0:T(8,128)(2,1)} %get-tuple-element.19) | copy-start | bytes 1572868
  36.8 115.5 %all-to-all-start = ((bf16[8,256,1024]{2,1,0:T(8,128)(2,1)}), bf16[8,256,1024]{2,1,0:T(8,128)(2,1)}, u32[]{:S(2)}, u32[]{:S(2)}) async-start(bf16[8,256,1024]{2,1,0:T(8,128)(2,1)} %bitcast.29), calls=%async_computation | async-start | bytes 8388608 | tf_op jit(solution)/shard_map/all_to_all | solution.py:276
  59.1 2.7 %copy-start.1 = (bf16[1024,3072]{1,0:T(8,128)(2,1)}, bf16[1024,3072]{1,0:T(8,128)(2,1)S(1)}, u32[]{:S(2)}) copy-start(bf16[1024,3072]{1,0:T(8,128)(2,1)S(1)} %convolution_convert_fusion.1.p_ref) | copy-start | bytes 18874372
  61.7 0.7 copy-start.2
  62.4 0.6 copy-start.3
  146.8 9.9 %copy-start.4 = (bf16[8,64,1024]{2,1,0:T(8,128)(2,1)S(1)}, bf16[8,64,1024]{2,1,0:T(8,128)(2,1)}, u32[]{:S(2)}) copy-start(bf16[8,64,1024]{2,1,0:T(8,128)(2,1)} %get-tuple-element.27) | copy-start | bytes 3145732
  152.3 29.7 %all-to-all-start.1 = ((bf16[8,64,1024]{2,1,0:T(8,128)(2,1)}), bf16[8,64,1024]{2,1,0:T(8,128)(2,1)}, u32[]{:S(2)}, u32[]{:S(2)}) async-start(bf16[8,64,1024]{2,1,0:T(8,128)(2,1)} %gather_fusion.1), calls=%async_computation.1 | async-start | bytes 2097152 | tf_op jit(solution)/shard_map/all_to_all | solution.py:276
  182.0 5.0 %slice-start = ((s8[6291456]{0:T(1024)(128)(4,1)}), s8[4194304]{0:T(1024)(128)(4,1)S(1)}, s32[]{:S(2)}) async-start(s8[6291456]{0:T(1024)(128)(4,1)} %bitcast.25), calls=%async_computation.2 | async-start | bytes 8388608
  182.0 5.0 %slice-start.1 = ((s8[6291456]{0:T(1024)(128)(4,1)}), s8[2097152]{0:T(1024)(128)(4,1)S(1)}, s32[]{:S(2)}) async-start(s8[6291456]{0:T(1024)(128)(4,1)} %bitcast.25), calls=%async_computation.3 | async-start | bytes 4194304
